TPU v7x, 128 devices: a whole 4x4x4 slice. The times are simulated.
128 devices in a mesh: sect: 16 (over x, z), rup: 8 (over y, core).
Axes of the slice: x: 4, y: 4, z: 4, core: 2. Of those that a mesh axis runs over, the one named last changes fastest.
Arguments:
- green_tensor: bfloat16 [64, 2, 6, 3, 1024, 128], P('sect', None, None, None, 'rup'), may hold values from -6 to 6
- slip_rate: bfloat16 [64, 32, 2, 1024, 128], P('rup', 'sect'), may hold values from -6 to 6
- moment_tensor: bfloat16 [64, 32, 6, 128], P('rup', 'sect'), may hold values from -0.02734375 to 0.02734375
- section_ids: int32 [64, 32], P('rup', 'sect'), may hold values from 0 to 15, as said below
- block_ids: int32 [64, 32], P('rup', 'sect'), may hold values from 0 to 3
Outputs:
- seismogram: float32 [64, 3, 2048], P('sect', None, 'rup')
Inputs may be any that keep to these rules, and one draw needn't show every extreme that they name: `section_ids`: among the 16 entries held by one device (one block of 8 ruptures times one block of 2 list positions), no section is named more than 2 times, and one section, the same for every device, is named exactly 2 times by every device.
All inputs are finite; a program needn't handle non-finite values.
Results may differ from a plain program's by a relative error of at most 0.0029.
Values may be sent and summed in bfloat16 or wider, within the bound.
No kernel may reach another device: no remote copies, remote signals or barrier semaphores. Data moves between devices by JAX's collectives and lax.ppermute only.
A program may use at most 128 MiB of HBM per device.

v0:
```python
import math

import jax
import jax.numpy as jnp
from jax import lax
from jax.sharding import PartitionSpec as P


def phase_table(freq_ids, time_ids, samples):
    phases = freq_ids[:, None] * time_ids[None, :] % samples
    angles = phases.astype(jnp.float32) * (2.0 * math.pi / samples)
    return (jnp.cos(angles), jnp.sin(angles))


def slot_spectra(arrived, green_tensor):
    slip_part, moment_part, labels = arrived
    sources = slip_part.shape[0]
    groups = math.gcd(8, sources)
    blocks_here = green_tensor.shape[0]

    def split_groups(values):
        return values.reshape((groups, sources // groups) + values.shape[1:])

    def one_group(pieces):
        slip_piece, moment_piece, label_piece = pieces
        weighted = (
            moment_piece[:, :, None, :, None, :].astype(jnp.float32)
            * slip_piece[:, :, :, None, :, :].astype(jnp.float32)
        ).astype(jnp.bfloat16)
        products = jnp.einsum(
            "akscfp,bgcjfp->aksbgjf", weighted, green_tensor, preferred_element_type=jnp.float32
        )
        block_of = label_piece[:, :, 0].astype(jnp.int32)
        chosen = (
            block_of[:, :, None] == jnp.arange(blocks_here, dtype=jnp.int32)[None, None, :]
        ).astype(jnp.float32)
        selected = jnp.einsum(
            "akb,aksbgjf->aksgjf", chosen, products, precision=lax.Precision.HIGHEST
        )
        real_part = selected[:, :, 0, 0] - selected[:, :, 1, 1]
        imag_part = selected[:, :, 0, 1] + selected[:, :, 1, 0]
        return jnp.stack([real_part, imag_part], axis=2)

    spectra = lax.map(
        one_group, (split_groups(slip_part), split_groups(moment_part), split_groups(labels))
    )
    spectra = spectra.reshape((sources,) + spectra.shape[2:])
    return (spectra, labels)


def body(green_tensor, slip_rate, moment_tensor, section_ids, block_ids):
    sect_devices = lax.axis_size("sect")
    rup_devices = lax.axis_size("rup")
    rupture_rows, list_cols = section_ids.shape
    entries = rupture_rows * list_cols
    capacity = (entries + sect_devices - 1) // sect_devices * 2
    frequencies = slip_rate.shape[3]
    points = slip_rate.shape[4]
    freq_slice = frequencies // rup_devices
    section_flat = section_ids.reshape(entries)
    block_flat = block_ids.reshape(entries)
    member = (section_flat[:, None] == jnp.arange(sect_devices, dtype=jnp.int32)[None, :]).astype(
        jnp.int32
    )
    earlier = jnp.cumsum(member, axis=0) - member
    position = jnp.sum(earlier * member, axis=1)
    target = section_flat * capacity + position
    matches = target[None, :] == jnp.arange(sect_devices * capacity, dtype=jnp.int32)[:, None]
    filled = jnp.any(matches, axis=1)
    source = jnp.sum(
        matches.astype(jnp.int32) * jnp.arange(entries, dtype=jnp.int32)[None, :], axis=1
    )
    flat_slip = slip_rate.reshape(entries, 2, frequencies, points)
    outgoing = jnp.where(
        filled[:, None, None, None], flat_slip[source], jnp.zeros((), jnp.bfloat16)
    )
    flat_moment = moment_tensor.reshape(entries, 6, points)
    out_moment = jnp.where(filled[:, None, None], flat_moment[source], jnp.zeros((), jnp.bfloat16))
    labels = jnp.stack([block_flat[source], source // list_cols], axis=1).astype(jnp.bfloat16)
    slip_send = outgoing.reshape(sect_devices, capacity, 2, rup_devices, freq_slice, points)
    slip_send = jnp.moveaxis(slip_send, 3, 1).reshape(
        sect_devices * rup_devices, capacity, 2, freq_slice, points
    )
    moment_send = jnp.broadcast_to(
        out_moment.reshape(sect_devices, 1, capacity, 6, points),
        (sect_devices, rup_devices, capacity, 6, points),
    )
    moment_send = moment_send.reshape(sect_devices * rup_devices, capacity, 6, points)
    label_send = jnp.broadcast_to(
        labels.reshape(sect_devices, 1, capacity, 2), (sect_devices, rup_devices, capacity, 2)
    )
    label_send = label_send.reshape(sect_devices * rup_devices, capacity, 2)
    spectra, slot_labels = slot_spectra(
        (
            lax.all_to_all(slip_send, ("sect", "rup"), split_axis=0, concat_axis=0, tiled=True),
            lax.all_to_all(moment_send, ("sect", "rup"), split_axis=0, concat_axis=0, tiled=True),
            lax.all_to_all(label_send, ("sect", "rup"), split_axis=0, concat_axis=0, tiled=True),
        ),
        green_tensor=green_tensor,
    )
    slots = sect_devices * rup_devices * capacity
    ruptures = rupture_rows * rup_devices
    flat_spectra = spectra.reshape(slots, 2, 3, freq_slice)
    flat_labels = slot_labels.reshape(slots, 2)
    slot_ids = jnp.arange(slots, dtype=jnp.int32)
    source_rup = slot_ids // capacity % rup_devices
    rupture_of = source_rup * rupture_rows + flat_labels[:, 1].astype(jnp.int32)
    owner_table = (rupture_of[:, None] == jnp.arange(ruptures, dtype=jnp.int32)[None, :]).astype(
        jnp.float32
    )
    section_part = jnp.einsum(
        "nr,nkjf->rkjf", owner_table, flat_spectra, precision=lax.Precision.HIGHEST
    )
    rup_index = lax.axis_index("rup")
    samples = 2 * frequencies
    per_device = samples // rup_devices
    summed = lax.psum_scatter(section_part, "sect", scatter_dimension=0, tiled=True)
    all_freqs = lax.all_gather(summed, "rup", axis=3, tiled=True)
    time_ids = rup_index * per_device + jnp.arange(per_device, dtype=jnp.int32)
    cosine_table, sine_table = phase_table(
        jnp.arange(frequencies, dtype=jnp.int32), time_ids, samples
    )
    seismogram = jnp.einsum(
        "rjf,ft->rjt", all_freqs[:, 0], cosine_table, precision=lax.Precision.HIGHEST
    )
    seismogram = seismogram - jnp.einsum(
        "rjf,ft->rjt", all_freqs[:, 1], sine_table, precision=lax.Precision.HIGHEST
    )
    seismogram = seismogram / math.sqrt(frequencies)
    return seismogram


def solution(mesh):
    placed = (
        P("sect", None, None, None, "rup", None),
        P("rup", "sect", None, None, None),
        P("rup", "sect", None, None),
        P("rup", "sect"),
        P("rup", "sect"),
    )
    return jax.shard_map(
        body, mesh=mesh, in_specs=placed, out_specs=P("sect", None, "rup"), check_vma=False
    )
```

profile of v0, /device:TPU:1, one launch (start us, length us, event | category | flops | bytes accessed | tf_op | source)
XLA Modules:
  0.0 661.3 jit_solution(8329417715365081421)
XLA Ops:
  6.5 0.8 copy.103
  7.9 0.8 copy.102
  8.7 0.7 gather_fusion
  9.9 0.7 broadcast_in_dim.35.clone
  10.5 11.5 %all-to-all-start = ((bf16[128,2,2]{2,1,0:T(2,128)(2,1)}), bf16[128,2,2]{2,1,0:T(2,128)(2,1)S(1)}, u32[]{:S(2)}, u32[]{:S(2)}) async-start(bf16[128,2,2]{2,1,0:T(2,128)(2,1)} %bitcast.19), calls=%async_computation | async-start | bytes 131072 | tf_op jit(solution)/shard_map/all_to_all | solution.py:97
  22.2 0.8 copy.109
  23.0 0.6 gather_fusion.1
  23.7 10.6 %gather_fusion.2 = bf16[32,2,1024,128]{3,2,1,0:T(8,128)(2,1)} fusion(bf16[16,2,1024,128]{3,2,1,0:T(8,128)(2,1)} %bitcast.111, s32[1024]{0:T(1024)S(1)} %pad_clamp_fusion), kind=kCustom, calls=%fused_computation.2 | custom fusion | bytes 33554560 | tf_op jit(solution)/shard_map/gather | solution.py:75
  34.3 1.0 broadcast_in_dim.45
  35.3 9.7 %all-to-all-start.1 = ((bf16[128,2,6,128]{3,1,2,0:T(2,128)(2,1)}), bf16[128,2,6,128]{3,1,2,0:T(2,128)(2,1)S(1)}, u32[]{:S(2)}, u32[]{:S(2)}) async-start(bf16[128,2,6,128]{3,1,2,0:T(2,128)(2,1)} %bitcast.27), calls=%async_computation.1 | async-start | bytes 786432 | tf_op jit(solution)/shard_map/all_to_all | solution.py:96
  45.0 8.3 %select_bitcast_fusion = bf16[16,8,2,2,128,128]{5,4,1,3,2,0:T(8,128)(2,1)S(1)} fusion(bf16[16,2,2,8,128,128]{5,4,3,2,1,0:T(8,128)(2,1)} %bitcast.110, pred[16,2]{1,0:T(8,128)(4,1)S(1)} %broadcast_in_dim.42), kind=kLoop, calls=%fused_computation.29 | loop fusion | flops 8388608 | bytes 33554464 | tf_op jit(solution)/shard_map/transpose | solution.py:81
  53.3 6.6 copy.113
  59.9 10.2 %all-to-all-start.2 = ((bf16[128,2,2,128,128]{4,3,2,1,0:T(8,128)(2,1)}), bf16[128,2,2,128,128]{4,3,2,1,0:T(8,128)(2,1)}, u32[]{:S(2)}, u32[]{:S(2)}) async-start(bf16[128,2,2,128,128]{4,3,2,1,0:T(8,128)(2,1)} %bitcast.109), calls=%async_computation.2 | async-start | bytes 33554432 | tf_op jit(solution)/shard_map/all_to_all | solution.py:95
  70.2 0.2 all-reduce.3.cloned.1.call-start
  70.4 8.2 %copy.117 = bf16[4,2,6,3,128,128]{5,0,2,3,1,4:T(4,128)(2,1)} copy(bf16[4,2,6,3,128,128]{5,4,3,2,1,0:T(8,128)(2,1)} %param.7) | data formatting | bytes 9437184 | tf_op jit(solution)/shard_map/while | solution.py:44
  79.0 223.6 %all-to-all-done.2 = bf16[128,2,2,128,128]{4,3,2,1,0:T(8,128)(2,1)} async-done(((bf16[128,2,2,128,128]{4,3,2,1,0:T(8,128)(2,1)}), bf16[128,2,2,128,128]{4,3,2,1,0:T(8,128)(2,1)}, u32[]{:S(2)}, u32[]{:S(2)}) %all-to-all-start.2) | async-done | bytes 16777248 | tf_op jit(solution)/shard_map/all_to_all | solution.py:95
  302.6 238.7 %while.10 = (s32[]{:T(128)}, f32[8,16,2,2,3,128]{5,4,3,2,1,0:T(4,128)S(1)}, bf16[8,16,2,2]{1,3,2,0:T(2,128)(2,1)S(1)}, bf16[8,16,2,6,128]{4,2,3,1,0:T(2,128)(2,1...) while((s32[]{:T(128)}, ...), condition=%wide.region_5.6_spmd, body=%wide.region_4.5_spmd.sunk | while | flops 318054560 | bytes 42910904 | solution.py:44
  302.6 1.9 constant_dynamic-slice_fusion.6
  304.5 1.2 fusion.70
  305.8 19.8 %fusion.72 = f32[16,2,2,4,2,3,128]{0,3,5,4,2,1,6:T(4,128)} fusion(bf16[4,2,6,3,128,128]{5,0,2,3,1,4:T(4,128)(2,1)S(1)} %copy-done, f32[16,2,2,128,128]{4,0,2,1,3:T(8,128)S(1)} %fusion.70, f32[16,2,6,128]{3,0,2,1:T(8,128)S(1)} %fusion.71), kind=kOutput, calls=%fused_computation.9.clone.1 | convolution fusion | flops 314572800 | bytes 9797632 | tf_op jit(solution)/shard_map/while/body/eval_jaxpr/akscfp,bgcjfp->aksbgjf/dot_general | solution.py:30
  325.6 5.5 copy.159
  331.4 0.9 fusion.74
  332.4 1.9 constant_dynamic-slice_fusion.6
  334.3 1.2 fusion.70
  335.6 19.8 %fusion.72 = f32[16,2,2,4,2,3,128]{0,3,5,4,2,1,6:T(4,128)} fusion(bf16[4,2,6,3,128,128]{5,0,2,3,1,4:T(4,128)(2,1)S(1)} %copy-done, f32[16,2,2,128,128]{4,0,2,1,3:T(8,128)S(1)} %fusion.70, f32[16,2,6,128]{3,0,2,1:T(8,128)S(1)} %fusion.71), kind=kOutput, calls=%fused_computation.9.clone.1 | convolution fusion | flops 314572800 | bytes 9797632 | tf_op jit(solution)/shard_map/while/body/eval_jaxpr/akscfp,bgcjfp->aksbgjf/dot_general | solution.py:30
  355.4 5.5 copy.159
  361.2 0.9 fusion.74
  362.2 1.9 constant_dynamic-slice_fusion.6
  364.1 1.2 fusion.70
  365.4 19.8 %fusion.72 = f32[16,2,2,4,2,3,128]{0,3,5,4,2,1,6:T(4,128)} fusion(bf16[4,2,6,3,128,128]{5,0,2,3,1,4:T(4,128)(2,1)S(1)} %copy-done, f32[16,2,2,128,128]{4,0,2,1,3:T(8,128)S(1)} %fusion.70, f32[16,2,6,128]{3,0,2,1:T(8,128)S(1)} %fusion.71), kind=kOutput, calls=%fused_computation.9.clone.1 | convolution fusion | flops 314572800 | bytes 9797632 | tf_op jit(solution)/shard_map/while/body/eval_jaxpr/akscfp,bgcjfp->aksbgjf/dot_general | solution.py:30
  385.3 5.5 copy.159
  391.0 0.9 fusion.74
  392.1 1.9 constant_dynamic-slice_fusion.6
  394.0 1.2 fusion.70
  395.3 19.8 %fusion.72 = f32[16,2,2,4,2,3,128]{0,3,5,4,2,1,6:T(4,128)} fusion(bf16[4,2,6,3,128,128]{5,0,2,3,1,4:T(4,128)(2,1)S(1)} %copy-done, f32[16,2,2,128,128]{4,0,2,1,3:T(8,128)S(1)} %fusion.70, f32[16,2,6,128]{3,0,2,1:T(8,128)S(1)} %fusion.71), kind=kOutput, calls=%fused_computation.9.clone.1 | convolution fusion | flops 314572800 | bytes 9797632 | tf_op jit(solution)/shard_map/while/body/eval_jaxpr/akscfp,bgcjfp->aksbgjf/dot_general | solution.py:30
  415.1 5.5 copy.159
  420.9 0.9 fusion.74
  421.9 1.9 constant_dynamic-slice_fusion.6
  423.8 1.2 fusion.70
  425.1 19.8 %fusion.72 = f32[16,2,2,4,2,3,128]{0,3,5,4,2,1,6:T(4,128)} fusion(bf16[4,2,6,3,128,128]{5,0,2,3,1,4:T(4,128)(2,1)S(1)} %copy-done, f32[16,2,2,128,128]{4,0,2,1,3:T(8,128)S(1)} %fusion.70, f32[16,2,6,128]{3,0,2,1:T(8,128)S(1)} %fusion.71), kind=kOutput, calls=%fused_computation.9.clone.1 | convolution fusion | flops 314572800 | bytes 9797632 | tf_op jit(solution)/shard_map/while/body/eval_jaxpr/akscfp,bgcjfp->aksbgjf/dot_general | solution.py:30
  444.9 5.5 copy.159
  450.7 0.9 fusion.74
  451.8 1.9 constant_dynamic-slice_fusion.6
  453.6 1.2 fusion.70
  454.9 19.8 %fusion.72 = f32[16,2,2,4,2,3,128]{0,3,5,4,2,1,6:T(4,128)} fusion(bf16[4,2,6,3,128,128]{5,0,2,3,1,4:T(4,128)(2,1)S(1)} %copy-done, f32[16,2,2,128,128]{4,0,2,1,3:T(8,128)S(1)} %fusion.70, f32[16,2,6,128]{3,0,2,1:T(8,128)S(1)} %fusion.71), kind=kOutput, calls=%fused_computation.9.clone.1 | convolution fusion | flops 314572800 | bytes 9797632 | tf_op jit(solution)/shard_map/while/body/eval_jaxpr/akscfp,bgcjfp->aksbgjf/dot_general | solution.py:30
  474.8 5.5 copy.159
  480.5 0.9 fusion.74
  481.6 1.9 constant_dynamic-slice_fusion.6
  483.5 1.2 fusion.70
  484.8 19.8 %fusion.72 = f32[16,2,2,4,2,3,128]{0,3,5,4,2,1,6:T(4,128)} fusion(bf16[4,2,6,3,128,128]{5,0,2,3,1,4:T(4,128)(2,1)S(1)} %copy-done, f32[16,2,2,128,128]{4,0,2,1,3:T(8,128)S(1)} %fusion.70, f32[16,2,6,128]{3,0,2,1:T(8,128)S(1)} %fusion.71), kind=kOutput, calls=%fused_computation.9.clone.1 | convolution fusion | flops 314572800 | bytes 9797632 | tf_op jit(solution)/shard_map/while/body/eval_jaxpr/akscfp,bgcjfp->aksbgjf/dot_general | solution.py:30
  504.6 5.5 copy.159
  510.4 0.9 fusion.74
  511.4 1.9 constant_dynamic-slice_fusion.6
  513.3 1.2 fusion.70
  514.6 19.8 %fusion.72 = f32[16,2,2,4,2,3,128]{0,3,5,4,2,1,6:T(4,128)} fusion(bf16[4,2,6,3,128,128]{5,0,2,3,1,4:T(4,128)(2,1)S(1)} %copy-done, f32[16,2,2,128,128]{4,0,2,1,3:T(8,128)S(1)} %fusion.70, f32[16,2,6,128]{3,0,2,1:T(8,128)S(1)} %fusion.71), kind=kOutput, calls=%fused_computation.9.clone.1 | convolution fusion | flops 314572800 | bytes 9797632 | tf_op jit(solution)/shard_map/while/body/eval_jaxpr/akscfp,bgcjfp->aksbgjf/dot_general | solution.py:30
  534.5 5.5 copy.159
  540.2 0.9 fusion.74
  541.2 1.1 fusion.31
  542.4 0.6 dynamic-slice
  543.7 86.8 %all-reduce.3.cloned.1.call-done = f32[64,2,3,128]{3,0,2,1:T(8,128)} async-done(((f32[64,2,3,128]{3,0,2,1:T(8,128)}), f32[64,2,3,128]{3,0,2,1:T(8,128)}) %all-reduce.3.cloned.1.call-update) | async-done | bytes 196624
  630.5 0.7 constant_dynamic-slice_fusion.3
  631.2 13.9 %all_gather.3 = f32[4,2,3,1024]{3,0,2,1:T(4,128)S(1)} all-gather(f32[4,2,3,128]{3,0,2,1:T(4,128)S(1)} %constant_dynamic-slice_fusion.3), channel_id=1, replica_groups=mesh['sect'=16,'rup'=8] {'rup'}, dimensions={3}, use_global_device_ids=true | all-gather | bytes 110592 | tf_op jit(solution)/shard_map/all_gather | solution.py:118
  645.1 4.4 fusion.24
  649.5 5.0 fusion.19
  (122 shorter events, 4.8 us)
Async XLA Ops:
  10.5 23.8 %all-to-all-start = ((bf16[128,2,2]{2,1,0:T(2,128)(2,1)}), bf16[128,2,2]{2,1,0:T(2,128)(2,1)S(1)}, u32[]{:S(2)}, u32[]{:S(2)}) async-start(bf16[128,2,2]{2,1,0:T(2,128)(2,1)} %bitcast.19), calls=%async_computation | async-start | bytes 131072 | tf_op jit(solution)/shard_map/all_to_all | solution.py:97
  35.3 24.6 %all-to-all-start.1 = ((bf16[128,2,6,128]{3,1,2,0:T(2,128)(2,1)}), bf16[128,2,6,128]{3,1,2,0:T(2,128)(2,1)S(1)}, u32[]{:S(2)}, u32[]{:S(2)}) async-start(bf16[128,2,6,128]{3,1,2,0:T(2,128)(2,1)} %bitcast.27), calls=%async_computation.1 | async-start | bytes 786432 | tf_op jit(solution)/shard_map/all_to_all | solution.py:96
  59.9 242.6 %all-to-all-start.2 = ((bf16[128,2,2,128,128]{4,3,2,1,0:T(8,128)(2,1)}), bf16[128,2,2,128,128]{4,3,2,1,0:T(8,128)(2,1)}, u32[]{:S(2)}, u32[]{:S(2)}) async-start(bf16[128,2,2,128,128]{4,3,2,1,0:T(8,128)(2,1)} %bitcast.109), calls=%async_computation.2 | async-start | bytes 33554432 | tf_op jit(solution)/shard_map/all_to_all | solution.py:95
  70.2 560.3 %all-reduce.3.cloned.1.call-start = ((), (), s32[]{:S(2)}) async-start(), calls=%async_computation.3 | async-start | bytes 393216
  302.6 239.9 %copy-start.1 = (u32[128]{0:T(128)S(1)}, u32[128]{0:T(128)}, u32[]{:S(2)}) copy-start(u32[128]{0:T(128)} %constant.102) | copy-start | bytes 1540
  302.6 3.2 copy-start
  332.4 3.2 copy-start
  362.2 3.2 copy-start
  392.1 3.2 copy-start
  421.9 3.2 copy-start
  451.7 3.2 copy-start
  481.6 3.2 copy-start
  511.4 3.2 copy-start
Sparse Core Ops, SparseCore 0:
  542.5 87.8 all-reduce.2
where the time goes:
time: 663 us; the launch traced here: 661 us
  waiting for transfers between devices  310 us (47%)
  matrix products  176 us (27%)
  local copies, waits for them, and re-layouts  93.9 us (14%)
  starting transfers between devices  31.7 us (5%)
  other arithmetic  20.2 us (3%)
  between operations  14.2 us (2%)
  blocking collectives  13.9 us (2%)
    all_to_all x1, waiting for transfers between devices, body(): lax.all_to_all(slip_send, ('sect', 'rup'), split_axis=0, concat_axis=0, t...  224 us
    dot_general x8, matrix products, one_group(): jnp.einsum('akscfp,bgcjfp->aksbgjf', weighted, green_tensor, preferred_el...  159 us
    unnamed x2, waiting for transfers between devices  86.8 us
    transpose x8, local copies, waits for them, and re-layouts, one_group(): jnp.einsum('akscfp,bgcjfp->aksbgjf', weighted, green_tensor, preferred_el...  44.4 us
    dynamic_slice x16, local copies, waits for them, and re-layouts, slot_spectra(): lax.map(one_group, (split_groups(slip_part), split_groups(moment_part), s...  15.4 us
    all_gather x1, blocking collectives, body(): all_freqs = lax.all_gather(summed, 'rup', axis=3, tiled=True)  13.9 us
  transfers between devices with their start and end apart: 4, of which 2 were waited for; matrix products, arithmetic and copies ran while one was open for 5% of the time, Pallas kernels for 0%

commit v1 on v0

v1 whole, which is shorter than its diff:
```python
import functools
import math

import jax
import jax.numpy as jnp
import numpy as np
from jax import lax
from jax.experimental import pallas as pl
from jax.experimental.pallas import tpu as pltpu
from jax.sharding import PartitionSpec as P

PARTS = (6, 2)
STEP = 16
LANES = 128


def phase_table(freq_ids, time_ids, samples):
    phases = freq_ids[:, None] * time_ids[None, :] % samples
    angles = phases.astype(jnp.float32) * (2.0 * math.pi / samples)
    return (jnp.cos(angles), jnp.sin(angles))


def split_kernel(slip_ref, *out_refs):
    lists, parts, devices = slip_ref.shape[1:4]
    for part in range(parts):
        for d in range(devices):
            turned = [
                jnp.swapaxes(slip_ref[:, l, part, d].astype(jnp.float32), 0, 1) for l in range(lists)
            ]
            turned = jnp.concatenate(turned, axis=1).astype(slip_ref.dtype)
            first = 0
            for out_ref in out_refs:
                count = out_ref.shape[2]
                out_ref[d, 0, :, part] = turned[first : first + count]
                first += count


def split(slip, counts, sects, some):
    rows, lists, parts, devices, sub, points = slip.shape
    steps = sects // some
    shapes = [(sects, devices // sects, count, parts, lists * rows, points) for count in counts]
    return pl.pallas_call(
        split_kernel,
        grid=(devices // sects, steps),
        in_specs=[
            pl.BlockSpec((rows, lists, parts, some, sub, points), lambda k, i: (0, 0, 0, k * steps + i, 0, 0))
        ],
        out_specs=[pl.BlockSpec((some, 1) + shape[2:], lambda k, i: (i, k, 0, 0, 0, 0)) for shape in shapes],
        out_shape=[jax.ShapeDtypeStruct(shape, slip.dtype) for shape in shapes],
        compiler_params=pltpu.CompilerParams(vmem_limit_bytes=60 * 2**20),
    )(slip)


def contract_kernel(width, blocks, sub, first, final, *refs):
    if final:
        slip_ref, moment_ref, green_ref, fold_ref, prev_ref, out_ref, acc_ref, sum_ref = refs
    else:
        slip_ref, moment_ref, green_ref, fold_ref, sum_ref, acc_ref = refs
    rups, sects, rows_per = moment_ref.shape[:3]
    comps = rows_per - 1
    entries, points = moment_ref.shape[3:]
    half = entries // 2
    cols = green_ref.shape[2]
    green = jnp.concatenate([green_ref[0, c] for c in range(comps)], axis=1)
    col = lax.broadcasted_iota(jnp.int32, (1, 1, 1, cols), 3)
    col_block = (col // width * blocks + col % blocks).astype(jnp.float32)
    acc_ref[...] = jnp.zeros(acc_ref.shape, jnp.float32)
    f = pl.program_id(0)

    @pl.when(f == 0)
    def _():
        sum_ref[...] = prev_ref[...] if final else jnp.zeros(sum_ref.shape, jnp.float32)

    def step(i, carry):
        some = pl.ds(i * STEP, STEP)
        ids = moment_ref[:, some, comps].astype(jnp.float32)
        mask = jnp.concatenate([ids] * (cols // points), axis=3) == col_block
        for part in range(2):
            slip = jnp.swapaxes(slip_ref[some, :, 0, part], 0, 1)
            weighted = jnp.concatenate(
                [
                    (slip * moment_ref[:, some, c]).reshape(rups * STEP * entries, points)
                    for c in range(comps)
                ],
                axis=1,
            )
            products = lax.dot_general(
                weighted, green, (((1,), (1,)), ((), ())), preferred_element_type=jnp.float32
            )
            kept = jnp.where(mask, products.reshape(rups, STEP, entries, cols), 0.0)
            kept = kept.reshape(rups, STEP, 2, half, cols)
            total = kept[:, 0, 0] + kept[:, 0, 1]
            for g in range(1, STEP):
                total = total + kept[:, g, 0] + kept[:, g, 1]
            acc_ref[part] += total
        return carry

    lax.fori_loop(0, sects // STEP, step, 0)
    spectrum = None
    for part in range(2):
        rest = acc_ref[part].reshape(rups * half, cols)
        for _ in range(3):
            piece = rest.astype(jnp.bfloat16)
            term = jnp.dot(piece, fold_ref[part], preferred_element_type=jnp.float32)
            spectrum = term if spectrum is None else spectrum + term
            rest = rest - piece.astype(jnp.float32)
    sum_ref[...] += pltpu.roll(spectrum, f + first, 1)
    if final:

        @pl.when(f == pl.num_programs(0) - 1)
        def _():
            owned = out_ref.shape[1]
            for s in range(sects):
                mine = sum_ref[s * owned : (s + 1) * owned]
                for k in range(rups):
                    out_ref[s * rups + k] = mine


def contract(slip, moment, green, fold, prev, first, width, blocks):
    sects, rups, freqs, _, entries, points = slip.shape
    sub = green.shape[0]
    cols = green.shape[2]
    ruptures = rups * entries // 2
    comps = moment.shape[2] - 1
    final = prev is not None
    in_specs = [
        pl.BlockSpec((sects, rups, 1, 2, entries, points), lambda f: (0, 0, f, 0, 0, 0)),
        pl.BlockSpec(moment.shape, lambda f: (0, 0, 0, 0, 0)),
        pl.BlockSpec((1,) + green.shape[1:], lambda f: (f + first, 0, 0, 0)),
        pl.BlockSpec(fold.shape, lambda f: (0, 0, 0)),
    ]
    args = [slip, moment, green, fold]
    scratch = [pltpu.VMEM((2, rups, entries // 2, cols), jnp.float32)]
    if final:
        in_specs.append(pl.BlockSpec(prev.shape, lambda f: (0, 0)))
        args.append(prev)
        shape = (sects * rups, ruptures // sects, LANES)
        scratch.append(pltpu.VMEM((ruptures, LANES), jnp.float32))
    else:
        shape = (ruptures, LANES)
    return pl.pallas_call(
        functools.partial(contract_kernel, width, blocks, sub, first, final),
        grid=(freqs,),
        in_specs=in_specs,
        out_specs=pl.BlockSpec(shape, lambda f: (0,) * len(shape)),
        out_shape=jax.ShapeDtypeStruct(shape, jnp.float32),
        scratch_shapes=scratch,
        compiler_params=pltpu.CompilerParams(vmem_limit_bytes=60 * 2**20),
        cost_estimate=pl.CostEstimate(
            flops=freqs * 4 * sects * rups * entries * comps * points * cols,
            bytes_accessed=freqs * (sects * rups * entries * points * 4 + comps * cols * points * 2),
            transcendentals=0,
        ),
    )(*args)


def fold_table(cols, blocks, sub):
    col = np.arange(cols)
    part, direction = col // blocks % 2, col // (2 * blocks) % 3
    out = np.arange(LANES)
    value = np.where((out < 6 * sub) & (out % sub == 0), out // sub, -1)
    same = (direction[:, None] == (value % 3)[None, :]) & (value >= 0)[None, :]
    equal = part[:, None] == (value // 3)[None, :]
    sign = np.where(value // 3 == 0, -1.0, 1.0)[None, :]
    real_slip = np.where(same & equal, 1.0, 0.0)
    imag_slip = np.where(same & ~equal, sign, 0.0)
    return jnp.asarray(np.stack([real_slip, imag_slip]), jnp.bfloat16)


def transform_table(first_time, times, frequencies, sects, rups, sub):
    samples = 2 * frequencies
    time_ids = first_time + jnp.arange(times, dtype=jnp.int32)
    base = np.arange(sects)[:, None] * sub + np.arange(rups)[None, :] * (frequencies // rups)
    base_cos, base_sin = phase_table(jnp.asarray(base.reshape(-1), jnp.int32), time_ids, samples)
    rest_cos, rest_sin = phase_table(jnp.arange(sub, dtype=jnp.int32), time_ids, samples)
    base_cos, base_sin, rest_cos, rest_sin = lax.optimization_barrier((base_cos, base_sin, rest_cos, rest_sin))
    cosine = rest_cos[:, None] * base_cos[None] - rest_sin[:, None] * base_sin[None]
    sine = rest_sin[:, None] * base_cos[None] + rest_cos[:, None] * base_sin[None]
    table = jnp.stack([cosine, -sine]) * (1.0 / math.sqrt(frequencies))
    table = table.reshape(2 * frequencies, times)
    high = table.astype(jnp.bfloat16)
    return high, (table - high.astype(jnp.float32)).astype(jnp.bfloat16)


def transform_kernel(sub, spectra_ref, high_ref, low_ref, out_ref, turned_ref, left_ref):
    dirs, owned = out_ref.shape[:2]
    devices = spectra_ref.shape[0]
    used = 2 * dirs * sub
    rows = left_ref.shape[0]
    for r in range(owned):
        turned_ref[r] = spectra_ref[:, r, :].T[:used]
    left_ref[...] = jnp.zeros(left_ref.shape, jnp.float32)
    for part in range(2):
        for f in range(sub):
            place = pl.ds((part * sub + f) * devices, devices)
            for r in range(owned):
                for j in range(dirs):
                    row = (part * dirs + j) * sub + f
                    left_ref[pl.ds(j * owned + r, 1), place] = turned_ref[r, pl.ds(row, 1), :]
    left = left_ref[...]
    high = left.astype(jnp.bfloat16)
    low = (left - high.astype(jnp.float32)).astype(jnp.bfloat16)
    both = jnp.concatenate([high, low], axis=0)
    first = jnp.dot(both, high_ref[...], preferred_element_type=jnp.float32)
    second = jnp.dot(high, low_ref[...], preferred_element_type=jnp.float32)
    result = first[:rows] + (first[rows:] + second)
    for j in range(dirs):
        out_ref[j] = result[j * owned : (j + 1) * owned]


def transform(spectra, high, low, dirs, sub):
    devices, owned, lanes = spectra.shape
    depth, times = high.shape
    return pl.pallas_call(
        functools.partial(transform_kernel, sub),
        out_shape=jax.ShapeDtypeStruct((dirs, owned, times), jnp.float32),
        scratch_shapes=[
            pltpu.VMEM((owned, 2 * dirs * sub, devices), jnp.float32),
            pltpu.VMEM((16, depth), jnp.float32),
        ],
        compiler_params=pltpu.CompilerParams(vmem_limit_bytes=16 * 2**20),
    )(spectra, high, low)


def body(green_tensor, slip_rate, moment_tensor, section_ids, block_ids):
    sects = lax.axis_size("sect")
    rups = lax.axis_size("rup")
    both = ("sect", "rup")
    blocks, _, comps, dirs, freq_slice, points = green_tensor.shape
    rup_rows, list_cols = section_ids.shape
    entries = rup_rows * list_cols
    frequencies = slip_rate.shape[3]
    sub = freq_slice // sects
    width = 2 * dirs * blocks
    cols = sects * width

    ids = (section_ids * blocks + block_ids).astype(jnp.bfloat16)
    ids = jnp.broadcast_to(ids.T.reshape(1, entries, 1), (1, entries, points))
    moment = jnp.transpose(moment_tensor, (2, 1, 0, 3)).reshape(comps, entries, points)
    moment = jnp.concatenate([moment, ids])
    moment = jnp.broadcast_to(moment[None], (sects,) + moment.shape)
    moment, green_tensor, slip_rate = lax.optimization_barrier((moment, green_tensor, slip_rate))
    moment = lax.all_to_all(moment, "sect", split_axis=0, concat_axis=0, tiled=True)

    green = green_tensor.reshape(blocks, 2, comps, dirs, sects, sub, points)
    green = jnp.transpose(green, (4, 5, 2, 3, 1, 0, 6)).reshape(sects, sub, comps, width, points)
    parts = split(slip_rate.reshape(rup_rows, list_cols, 2, rups * sects, sub, points), PARTS, sects, 8)
    green, moment, *parts = lax.optimization_barrier((green, moment, *parts))
    moment = lax.all_gather(moment, "rup", axis=0)
    green = lax.all_to_all(green, "sect", split_axis=0, concat_axis=0, tiled=True)
    green = jnp.transpose(green, (1, 2, 0, 3, 4)).reshape(sub, comps, cols, points)

    fold = fold_table(cols, blocks, sub)
    first_time = lax.axis_index("rup") * (2 * frequencies // rups)
    spectrum = None
    first = 0
    before = green
    for i, part in enumerate(parts):
        if i == 0:
            part, before, moment = lax.optimization_barrier((part, before, moment))
        else:
            part, before = lax.optimization_barrier((part, before))
        arrived = part.reshape((sects * rups,) + part.shape[2:])
        arrived = lax.all_to_all(arrived, both, split_axis=0, concat_axis=0, tiled=True)
        if i == 0:
            green = before
        else:
            spectrum = contract(before, moment, green, fold, spectrum, done, width, blocks)
        done = first
        before = arrived.reshape(part.shape)
        first += part.shape[2]
    first_time, before = lax.optimization_barrier((first_time, before))
    send = contract(before, moment, green, fold, spectrum, done, width, blocks)
    high, low = transform_table(first_time, 2 * frequencies // rups, frequencies, sects, rups, sub)

    all_freqs = lax.all_to_all(send, both, split_axis=0, concat_axis=0, tiled=True)
    return jnp.swapaxes(transform(all_freqs, high, low, dirs, sub), 0, 1)


def solution(mesh):
    placed = (
        P("sect", None, None, None, "rup", None),
        P("rup", "sect", None, None, None),
        P("rup", "sect", None, None),
        P("rup", "sect"),
        P("rup", "sect"),
    )
    return jax.shard_map(
        body, mesh=mesh, in_specs=placed, out_specs=P("sect", None, "rup"), check_vma=False
    )
```

time: 663 us -> 262 us (0.40)
  waiting for transfers between devices: 310 us -> 14.8 us
  matrix products: 176 us -> 0 us
  blocking collectives: 13.9 us -> 145 us
  local copies, waits for them, and re-layouts: 93.9 us -> 14.8 us
  Pallas kernels: 0 us -> 51.2 us
  other arithmetic: 20.2 us -> 2.06 us
  starting transfers between devices: 31.7 us -> 19.7 us
    all_to_all x3, waiting for transfers between devices: 224 us -> 14.8 us  [the longest x1 10.1 us: body(): lax.all_to_all(send, both, split_axis=0, concat_axis=0, tiled=True)]
    dot_general x19 -> x0, matrix products: 176 us -> none  [the longest x8 159 us: one_group(): jnp.einsum('akscfp,bgcjfp->aksbgjf', weighted, green_tensor, preferred_el...]
    all_to_all x0 -> x2, blocking collectives: none -> 145 us  [the longest x1 84.6 us: body(): lax.all_to_all(arrived, both, split_axis=0, concat_axis=0, tiled=True)]
    unnamed x2 -> x1, waiting for transfers between devices: 86.8 us -> 0.02 us
    pallas_call x0 -> x4, Pallas kernels: none -> 51.2 us  [the longest x2 36.5 us: contract(): pl.pallas_call(functools.partial(contract_kernel, width, blocks, sub, fir...]
    transpose x9 -> x1, local copies, waits for them, and re-layouts: 51 us -> 3.42 us  [body(): jnp.transpose(green, (1, 2, 0, 3, 4)).reshape(sub, comps, cols, points)]
    dynamic_slice x16 -> x0, local copies, waits for them, and re-layouts: 15.4 us -> none  [slot_spectra(): lax.map(one_group, (split_groups(slip_part), split_groups(moment_part), s...]
    all_gather x1 -> x0, blocking collectives: 13.9 us -> none  [body(): all_freqs = lax.all_gather(summed, 'rup', axis=3, tiled=True)]
  transfers between devices with their start and end apart: 4 -> 4, of which waited for: 2 -> 2; matrix products, arithmetic and copies ran while one was open for 5% -> 5% of each run, Pallas kernels for 0% -> 15%
where the time goes in v1:
time: 262 us; the launch traced here: 261 us
  blocking collectives  145 us (55%)
  Pallas kernels  51.2 us (20%)
  starting transfers between devices  19.7 us (8%)
  local copies, waits for them, and re-layouts  14.8 us (6%)
  waiting for transfers between devices  14.8 us (6%)
  between operations  13.5 us (5%)
    all_to_all x1, blocking collectives, body(): lax.all_to_all(arrived, both, split_axis=0, concat_axis=0, tiled=True)  84.6 us
    all_to_all x1, blocking collectives, body(): lax.all_to_all(green, 'sect', split_axis=0, concat_axis=0, tiled=True)  60.5 us
    pallas_call x2, Pallas kernels, contract(): pl.pallas_call(functools.partial(contract_kernel, width, blocks, sub, fir...  36.5 us
    pallas_call x1, Pallas kernels, split(): pl.pallas_call(split_kernel, grid=(devices // sects, steps), in_specs=[pl...  13.5 us
    all_to_all x1, waiting for transfers between devices, body(): lax.all_to_all(send, both, split_axis=0, concat_axis=0, tiled=True)  10.1 us
    all_to_all x1, starting transfers between devices, body(): lax.all_to_all(moment, 'sect', split_axis=0, concat_axis=0, tiled=True)  8.43 us
    reshape x1, local copies, waits for them, and re-layouts, body(): green = green_tensor.reshape(blocks, 2, comps, dirs, sects, sub, points)  8.18 us
    all_to_all x1, starting transfers between devices, body(): lax.all_to_all(arrived, both, split_axis=0, concat_axis=0, tiled=True)  6.16 us
  transfers between devices with their start and end apart: 4, of which 2 were waited for; matrix products, arithmetic and copies ran while one was open for 5% of the time, Pallas kernels for 15%

profile of v1, /device:TPU:1, one launch (start us, length us, event | category | flops | bytes accessed | tf_op | source)
XLA Modules:
  0.0 261.1 jit_solution(5950629103045771229)
XLA Ops:
  6.5 0.7 copy.15
  7.3 0.7 fusion.14
  8.0 0.1 broadcast_in_dim.6
  8.1 0.1 broadcast_in_dim.7
  8.1 0.8 broadcast_in_dim.8
  9.0 8.4 %all-to-all-start = ((bf16[16,7,16,128]{3,2,1,0:T(8,128)(2,1)}), bf16[16,7,16,128]{3,2,1,0:T(8,128)(2,1)S(1)}, u32[]{:S(2)}, u32[]{:S(2)}) async-start(bf16[16,7,16,128]{3,2,1,0:T(8,128)(2,1)} %broadcast_in_dim.8), calls=%async_computation | async-start | bytes 917504 | tf_op jit(solution)/shard_map/all_to_all | solution.py:243
  17.4 0.0 all-gather.3.cloned.1.call-start
  17.5 13.5 %shard_map.73 = (bf16[16,8,6,2,16,128]{5,4,3,2,1,0:T(8,128)(2,1)}, bf16[16,8,2,2,16,128]{5,4,3,2,1,0:T(8,128)(2,1)}) custom-call(bf16[8,2,2,128,8,128]{5,4,3,2,1,0:T(8,128)(2,1)} %bitcast.28), custom_call_target="tpu_custom_call" | custom-call | tf_op jit(solution)/shard_map/pallas_call | solution.py:42
  31.0 8.2 %copy.12 = bf16[4,2,6,3,16,8,128]{6,0,1,3,2,5,4:T(4,128)(2,1)} copy(bf16[4,2,6,3,16,8,128]{6,5,4,3,2,1,0:T(8,128)(2,1)} %bitcast.31) | data formatting | bytes 9437184 | tf_op jit(solution)/shard_map/reshape | solution.py:245
  39.2 0.0 all-to-all-done
  39.2 0.0 copy-start.1
  39.2 0.8 copy-done.1
  40.0 0.0 all-gather.3.cloned.1.call-update
  40.0 60.5 %all_to_all.25 = bf16[16,8,6,24,128]{4,3,2,1,0:T(8,128)(2,1)S(1)} all-to-all(bf16[16,8,6,24,128]{4,3,2,1,0:T(8,128)(2,1)} %bitcast.26), channel_id=1, replica_groups=mesh['sect'=16,'rup'=8] {'sect'}, dimensions={0} | all-to-all | bytes 9437184 | tf_op jit(solution)/shard_map/all_to_all | solution.py:250
  100.5 3.4 %copy.13 = bf16[8,6,16,24,128]{4,3,2,1,0:T(8,128)(2,1)} copy(bf16[8,6,16,24,128]{4,3,1,0,2:T(8,128)(2,1)S(1)} %bitcast.27) | data formatting | bytes 9437184 | tf_op jit(solution)/shard_map/transpose | solution.py:251
  103.9 0.0 all-gather.3.cloned.1.call-done
  103.9 84.6 %all_to_all.26 = bf16[128,6,2,16,128]{4,3,2,1,0:T(8,128)(2,1)} all-to-all(bf16[128,6,2,16,128]{4,3,2,1,0:T(8,128)(2,1)} %bitcast.29), channel_id=1, replica_groups=mesh['sect'=16,'rup'=8] {'sect','rup'}, dimensions={0} | all-to-all | bytes 12582912 | tf_op jit(solution)/shard_map/all_to_all | solution.py:264
  188.5 6.2 %all-to-all-start.3 = ((bf16[128,2,2,16,128]{4,3,2,1,0:T(8,128)(2,1)}), bf16[128,2,2,16,128]{4,3,2,1,0:T(8,128)(2,1)S(1)}, u32[]{:S(2)}, u32[]{:S(2)}) async-start(bf16[128,2,2,16,128]{4,3,2,1,0:T(8,128)(2,1)} %bitcast.12), calls=%async_computation.3 | async-start | bytes 4194304 | tf_op jit(solution)/shard_map/all_to_all | solution.py:264
  194.7 0.0 copy-start.2
  194.7 25.6 %shard_map.74.refs_4_ = f32[64,128]{1,0:T(8,128)} custom-call(bf16[16,8,6,2,16,128]{5,4,3,2,1,0:T(8,128)(2,1)} %bitcast.30, bf16[8,16,7,16,128]{4,3,2,1,0:T(8,128)(2,1)} %bitcast.36, bf16[8,6,384,128]{3,2,1,0:T(8,128)(2,1)} %bitcast.32, bf16[2,384,128]{2,1,0:T(8,128)(2,1)} %constant.40.clone.refs_3_), custom_call_target="tpu_custom_call" | custom-call | flops 14495514624 | bytes 9830400 | tf_op jit(solution)/shard_map/pallas_call | solution.py:141
  220.3 4.7 %all-to-all-done.3 = bf16[128,2,2,16,128]{4,3,2,1,0:T(8,128)(2,1)S(1)} async-done(((bf16[128,2,2,16,128]{4,3,2,1,0:T(8,128)(2,1)}), bf16[128,2,2,16,128]{4,3,2,1,0:T(8,128)(2,1)S(1)}, u32[]{:S(2)}, u32[]{:S(2)}) %all-to-all-start.3) | async-done | bytes 2097184 | tf_op jit(solution)/shard_map/all_to_all | solution.py:264
  225.1 0.0 copy-start
  225.1 0.1 fusion.12
  225.1 0.0 copy-done.2
  225.1 0.6 fusion.4
  225.7 0.7 copy-done
  226.4 10.9 %shard_map.75 = f32[128,4,128]{2,1,0:T(4,128)} custom-call(bf16[16,8,2,2,16,128]{5,4,3,2,1,0:T(8,128)(2,1)} %bitcast.34, bf16[8,16,7,16,128]{4,3,2,1,0:T(8,128)(2,1)} %bitcast.37, bf16[8,6,384,128]{3,2,1,0:T(8,128)(2,1)} %bitcast.33, bf16[2,384,128]{2,1,0:T(8,128)(2,1)} %constant.40.clone.refs_3_, f32[64,128]{1,0:T(8,128)} %shard_map.74.refs_4_), custom_call_target="tpu_custom_call" | custom-call | flops 4831838208 | bytes 3276800 | tf_op jit(solution)/shard_map/pallas_call | solution.py:141
  237.2 5.0 %all-to-all-start.4 = ((f32[128,4,128]{2,1,0:T(4,128)}), f32[128,4,128]{2,1,0:T(4,128)S(1)}, u32[]{:S(2)}, u32[]{:S(2)}) async-start(f32[128,4,128]{2,1,0:T(4,128)} %shard_map.75), calls=%async_computation.4 | async-start | bytes 524288 | tf_op jit(solution)/shard_map/all_to_all | solution.py:276
  242.3 0.3 multiply_subtract_fusion
  242.5 0.2 maximum_multiply_fusion
  242.7 0.3 fusion
  243.0 10.1 %all-to-all-done.4.spectra_ref = f32[128,4,128]{2,1,0:T(4,128)S(1)} async-done(((f32[128,4,128]{2,1,0:T(4,128)}), f32[128,4,128]{2,1,0:T(4,128)S(1)}, u32[]{:S(2)}, u32[]{:S(2)}) %all-to-all-start.4) | async-done | bytes 262176 | tf_op jit(solution)/shard_map/all_to_all | solution.py:276
  253.1 1.2 shard_map.76
  (2 shorter events, 0.0 us)
Async XLA Ops:
  9.0 30.2 %all-to-all-start = ((bf16[16,7,16,128]{3,2,1,0:T(8,128)(2,1)}), bf16[16,7,16,128]{3,2,1,0:T(8,128)(2,1)S(1)}, u32[]{:S(2)}, u32[]{:S(2)}) async-start(bf16[16,7,16,128]{3,2,1,0:T(8,128)(2,1)} %broadcast_in_dim.8), calls=%async_computation | async-start | bytes 917504 | tf_op jit(solution)/shard_map/all_to_all | solution.py:243
  17.4 86.5 %all-gather.3.cloned.1.call-start = ((), (), s32[]{:S(2)}) async-start(), calls=%async_computation.5 | async-start | bytes 4128768 | tf_op jit(solution)/shard_map/all_gather | solution.py:249
  39.2 0.8 copy-start.1
  188.5 36.5 %all-to-all-start.3 = ((bf16[128,2,2,16,128]{4,3,2,1,0:T(8,128)(2,1)}), bf16[128,2,2,16,128]{4,3,2,1,0:T(8,128)(2,1)S(1)}, u32[]{:S(2)}, u32[]{:S(2)}) async-start(bf16[128,2,2,16,128]{4,3,2,1,0:T(8,128)(2,1)} %bitcast.12), calls=%async_computation.3 | async-start | bytes 4194304 | tf_op jit(solution)/shard_map/all_to_all | solution.py:264
  194.7 30.5 %copy-start.2 = (s32[128]{0:T(128)S(1)}, s32[128]{0:T(128)}, u32[]{:S(2)}) copy-start(s32[128]{0:T(128)} %constant.41.clone) | copy-start | bytes 1540
  225.1 1.3 copy-start
  237.2 15.8 %all-to-all-start.4 = ((f32[128,4,128]{2,1,0:T(4,128)}), f32[128,4,128]{2,1,0:T(4,128)S(1)}, u32[]{:S(2)}, u32[]{:S(2)}) async-start(f32[128,4,128]{2,1,0:T(4,128)} %shard_map.75), calls=%async_computation.4 | async-start | bytes 524288 | tf_op jit(solution)/shard_map/all_to_all | solution.py:276
Sparse Core Ops, SparseCore 0:
  40.1 32.3 all-gather.2

commit v2 on v1

--- a/solution.py
+++ b/solution.py
@@ -12,6 +12,7 @@
 PARTS = (6, 2)
 STEP = 16
 LANES = 128
+PAD = 1
 
 
 def phase_table(freq_ids, time_ids, samples):
@@ -20,35 +21,67 @@
     return (jnp.cos(angles), jnp.sin(angles))
 
 
-def split_kernel(slip_ref, *out_refs):
-    lists, parts, devices = slip_ref.shape[1:4]
+def load_rows(in_ref, wide_ref):
+    rows = in_ref.shape[0]
+    apart = wide_ref.shape[0] // rows
+    for r in range(rows):
+        block = in_ref[r].astype(jnp.float32).reshape(-1, in_ref.shape[-1])
+        wide_ref[pl.ds(r * apart, block.shape[0])] = block
+    return rows, apart
+
+
+def split_slip_kernel(slip_ref, *refs):
+    out_refs, wide_ref = refs[:-1], refs[-1]
+    rows, apart = load_rows(slip_ref, wide_ref)
+    lists, parts, devices, sub = slip_ref.shape[1:5]
     for part in range(parts):
         for d in range(devices):
-            turned = [
-                jnp.swapaxes(slip_ref[:, l, part, d].astype(jnp.float32), 0, 1) for l in range(lists)
-            ]
-            turned = jnp.concatenate(turned, axis=1).astype(slip_ref.dtype)
-            first = 0
+            f = 0
             for out_ref in out_refs:
-                count = out_ref.shape[2]
-                out_ref[d, 0, :, part] = turned[first : first + count]
-                first += count
-
-
-def split(slip, counts, sects, some):
+                for i in range(out_ref.shape[2]):
+                    places = [((l * parts + part) * devices + d) * sub + f for l in range(lists)]
+                    turned = [wide_ref[pl.ds(place, rows, stride=apart)] for place in places]
+                    out_ref[d, 0, i, part] = jnp.concatenate(turned, axis=0).astype(slip_ref.dtype)
+                    f += 1
+
+
+def split_slip(slip, counts, sects):
     rows, lists, parts, devices, sub, points = slip.shape
-    steps = sects // some
     shapes = [(sects, devices // sects, count, parts, lists * rows, points) for count in counts]
     return pl.pallas_call(
-        split_kernel,
-        grid=(devices // sects, steps),
-        in_specs=[
-            pl.BlockSpec((rows, lists, parts, some, sub, points), lambda k, i: (0, 0, 0, k * steps + i, 0, 0))
-        ],
-        out_specs=[pl.BlockSpec((some, 1) + shape[2:], lambda k, i: (i, k, 0, 0, 0, 0)) for shape in shapes],
+        split_slip_kernel,
+        grid=(devices // sects,),
+        in_specs=[pl.BlockSpec((rows, lists, parts, sects, sub, points), lambda k: (0, 0, 0, k, 0, 0))],
+        out_specs=[pl.BlockSpec((sects, 1) + shape[2:], lambda k: (0, k, 0, 0, 0, 0)) for shape in shapes],
         out_shape=[jax.ShapeDtypeStruct(shape, slip.dtype) for shape in shapes],
+        scratch_shapes=[pltpu.VMEM((rows * (lists * parts * sects * sub + PAD), points), jnp.float32)],
         compiler_params=pltpu.CompilerParams(vmem_limit_bytes=60 * 2**20),
     )(slip)
+
+
+def split_green_kernel(green_ref, out_ref, wide_ref):
+    rows, apart = load_rows(green_ref, wide_ref)
+    comps, dirs, sects, sub = green_ref.shape[1:5]
+    for s in range(sects):
+        for c in range(comps):
+            for f in range(sub):
+                places = [((c * dirs + j) * sects + s) * sub + f for j in range(dirs)]
+                turned = [wide_ref[pl.ds(place, rows, stride=apart)] for place in places]
+                out_ref[s, f, c] = jnp.concatenate(turned, axis=0).astype(green_ref.dtype)
+
+
+def split_green(green, sects):
+    rows, comps, dirs, _, sub, points = green.shape
+    shape = (sects, sub, comps, dirs * rows, points)
+    return pl.pallas_call(
+        split_green_kernel,
+        grid=(comps,),
+        in_specs=[pl.BlockSpec((rows, 1, dirs, sects, sub, points), lambda c: (0, c, 0, 0, 0, 0))],
+        out_specs=pl.BlockSpec((sects, sub, 1) + shape[3:], lambda c: (0, 0, c, 0, 0)),
+        out_shape=jax.ShapeDtypeStruct(shape, green.dtype),
+        scratch_shapes=[pltpu.VMEM((rows * (dirs * sects * sub + PAD), points), jnp.float32)],
+        compiler_params=pltpu.CompilerParams(vmem_limit_bytes=60 * 2**20),
+    )(green)
 
 
 def contract_kernel(width, blocks, sub, first, final, *refs):
@@ -60,10 +93,10 @@
     comps = rows_per - 1
     entries, points = moment_ref.shape[3:]
     half = entries // 2
-    cols = green_ref.shape[2]
-    green = jnp.concatenate([green_ref[0, c] for c in range(comps)], axis=1)
+    cols = sects * width
+    green = jnp.concatenate([green_ref[:, 0, c].reshape(cols, points) for c in range(comps)], axis=1)
     col = lax.broadcasted_iota(jnp.int32, (1, 1, 1, cols), 3)
-    col_block = (col // width * blocks + col % blocks).astype(jnp.float32)
+    col_block = (col // width * blocks + col % (2 * blocks) // 2).astype(jnp.float32)
     acc_ref[...] = jnp.zeros(acc_ref.shape, jnp.float32)
     f = pl.program_id(0)
 
@@ -118,15 +151,15 @@
 
 def contract(slip, moment, green, fold, prev, first, width, blocks):
     sects, rups, freqs, _, entries, points = slip.shape
-    sub = green.shape[0]
-    cols = green.shape[2]
+    sub = green.shape[1]
+    cols = sects * width
     ruptures = rups * entries // 2
     comps = moment.shape[2] - 1
     final = prev is not None
     in_specs = [
         pl.BlockSpec((sects, rups, 1, 2, entries, points), lambda f: (0, 0, f, 0, 0, 0)),
         pl.BlockSpec(moment.shape, lambda f: (0, 0, 0, 0, 0)),
-        pl.BlockSpec((1,) + green.shape[1:], lambda f: (f + first, 0, 0, 0)),
+        pl.BlockSpec((sects, 1) + green.shape[2:], lambda f: (0, f + first, 0, 0, 0)),
         pl.BlockSpec(fold.shape, lambda f: (0, 0, 0)),
     ]
     args = [slip, moment, green, fold]
@@ -156,7 +189,7 @@
 
 def fold_table(cols, blocks, sub):
     col = np.arange(cols)
-    part, direction = col // blocks % 2, col // (2 * blocks) % 3
+    part, direction = col % 2, col // (2 * blocks) % 3
     out = np.arange(LANES)
     value = np.where((out < 6 * sub) & (out % sub == 0), out // sub, -1)
     same = (direction[:, None] == (value % 3)[None, :]) & (value >= 0)[None, :]
@@ -178,8 +211,8 @@
     sine = rest_sin[:, None] * base_cos[None] + rest_cos[:, None] * base_sin[None]
     table = jnp.stack([cosine, -sine]) * (1.0 / math.sqrt(frequencies))
     table = table.reshape(2 * frequencies, times)
-    high = table.astype(jnp.bfloat16)
-    return high, (table - high.astype(jnp.float32)).astype(jnp.bfloat16)
+    high = lax.reduce_precision(table, 8, 7)
+    return high.astype(jnp.bfloat16), (table - high).astype(jnp.bfloat16)
 
 
 def transform_kernel(sub, spectra_ref, high_ref, low_ref, out_ref, turned_ref, left_ref):
@@ -242,13 +275,11 @@
     moment, green_tensor, slip_rate = lax.optimization_barrier((moment, green_tensor, slip_rate))
     moment = lax.all_to_all(moment, "sect", split_axis=0, concat_axis=0, tiled=True)
 
-    green = green_tensor.reshape(blocks, 2, comps, dirs, sects, sub, points)
-    green = jnp.transpose(green, (4, 5, 2, 3, 1, 0, 6)).reshape(sects, sub, comps, width, points)
-    parts = split(slip_rate.reshape(rup_rows, list_cols, 2, rups * sects, sub, points), PARTS, sects, 8)
+    green = split_green(green_tensor.reshape(blocks * 2, comps, dirs, sects, sub, points), sects)
+    parts = split_slip(slip_rate.reshape(rup_rows, list_cols, 2, rups * sects, sub, points), PARTS, sects)
     green, moment, *parts = lax.optimization_barrier((green, moment, *parts))
     moment = lax.all_gather(moment, "rup", axis=0)
     green = lax.all_to_all(green, "sect", split_axis=0, concat_axis=0, tiled=True)
-    green = jnp.transpose(green, (1, 2, 0, 3, 4)).reshape(sub, comps, cols, points)
 
     fold = fold_table(cols, blocks, sub)
     first_time = lax.axis_index("rup") * (2 * frequencies // rups)
@@ -269,8 +300,8 @@
         done = first
         before = arrived.reshape(part.shape)
         first += part.shape[2]
-    first_time, before = lax.optimization_barrier((first_time, before))
     send = contract(before, moment, green, fold, spectrum, done, width, blocks)
+    first_time, send = lax.optimization_barrier((first_time, send))
     high, low = transform_table(first_time, 2 * frequencies // rups, frequencies, sects, rups, sub)
 
     all_freqs = lax.all_to_all(send, both, split_axis=0, concat_axis=0, tiled=True)

time: 262 us -> 254 us (0.969)
  local copies, waits for them, and re-layouts: 14.8 us -> 3.84 us
  Pallas kernels: 51.2 us -> 54.1 us
    reshape x1 -> x0, local copies, waits for them, and re-layouts: 8.18 us -> none  [body(): green = green_tensor.reshape(blocks, 2, comps, dirs, sects, sub, points)]
    transpose x1 -> x0, local copies, waits for them, and re-layouts: 3.42 us -> none  [body(): jnp.transpose(green, (1, 2, 0, 3, 4)).reshape(sub, comps, cols, points)]
    pallas_call x1 -> x2, Pallas kernels: 13.5 us -> 16.4 us  [the longest x1 9.81 us: split_slip(): pl.pallas_call(split_slip_kernel, grid=(devices // sects,), in_specs=[pl....]
  transfers between devices with their start and end apart: 4 -> 4, of which waited for: 2 -> 2; matrix products, arithmetic and copies ran while one was open for 5% -> 0% of each run, Pallas kernels for 15% -> 17%
where the time goes in v2:
time: 254 us; the launch traced here: 253 us
  blocking collectives  145 us (57%)
  Pallas kernels  54.1 us (21%)
  starting transfers between devices  19.7 us (8%)
  waiting for transfers between devices  14.7 us (6%)
  between operations  13.5 us (5%)
  local copies, waits for them, and re-layouts  3.84 us (2%)
    all_to_all x1, blocking collectives, body(): lax.all_to_all(arrived, both, split_axis=0, concat_axis=0, tiled=True)  84.6 us
    all_to_all x1, blocking collectives, body(): lax.all_to_all(green, 'sect', split_axis=0, concat_axis=0, tiled=True)  60.6 us
    pallas_call x2, Pallas kernels, contract(): pl.pallas_call(functools.partial(contract_kernel, width, blocks, sub, fir...  36.5 us
    all_to_all x1, waiting for transfers between devices, body(): lax.all_to_all(send, both, split_axis=0, concat_axis=0, tiled=True)  9.97 us
    pallas_call x1, Pallas kernels, split_slip(): pl.pallas_call(split_slip_kernel, grid=(devices // sects,), in_specs=[pl....  9.81 us
    all_to_all x1, starting transfers between devices, body(): lax.all_to_all(moment, 'sect', split_axis=0, concat_axis=0, tiled=True)  8.43 us
    pallas_call x1, Pallas kernels, split_green(): pl.pallas_call(split_green_kernel, grid=(comps,), in_specs=[pl.BlockSpec(...  6.58 us
    all_to_all x1, starting transfers between devices, body(): lax.all_to_all(arrived, both, split_axis=0, concat_axis=0, tiled=True)  6.15 us
  transfers between devices with their start and end apart: 4, of which 2 were waited for; matrix products, arithmetic and copies ran while one was open for 0% of the time, Pallas kernels for 17%

profile of v2, /device:TPU:1, one launch (start us, length us, event | category | flops | bytes accessed | tf_op | source)
XLA Modules:
  0.0 253.1 jit_solution(15366694500813680303)
XLA Ops:
  6.5 0.7 copy.11
  7.3 0.7 fusion.14
  8.0 0.1 broadcast_in_dim.6
  8.1 0.1 broadcast_in_dim.7
  8.1 0.8 broadcast_in_dim.8
  9.0 8.4 %all-to-all-start = ((bf16[16,7,16,128]{3,2,1,0:T(8,128)(2,1)}), bf16[16,7,16,128]{3,2,1,0:T(8,128)(2,1)S(1)}, u32[]{:S(2)}, u32[]{:S(2)}) async-start(bf16[16,7,16,128]{3,2,1,0:T(8,128)(2,1)} %broadcast_in_dim.8), calls=%async_computation | async-start | bytes 917504 | tf_op jit(solution)/shard_map/all_to_all | solution.py:276
  17.4 0.0 all-gather.3.cloned.1.call-start
  17.5 9.8 %shard_map.74 = (bf16[16,8,6,2,16,128]{5,4,3,2,1,0:T(8,128)(2,1)}, bf16[16,8,2,2,16,128]{5,4,3,2,1,0:T(8,128)(2,1)}) custom-call(bf16[8,2,2,128,8,128]{5,4,3,2,1,0:T(8,128)(2,1)} %bitcast.18), custom_call_target="tpu_custom_call" | custom-call | tf_op jit(solution)/shard_map/pallas_call | solution.py:51
  27.3 6.6 %shard_map.73 = bf16[16,8,6,24,128]{4,3,2,1,0:T(8,128)(2,1)} custom-call(bf16[8,6,3,16,8,128]{5,4,3,2,1,0:T(8,128)(2,1)} %bitcast.21), custom_call_target="tpu_custom_call" | custom-call | tf_op jit(solution)/shard_map/pallas_call | solution.py:76
  33.9 0.0 all-to-all-done
  33.9 0.0 copy-start.1
  33.9 0.8 copy-done.1
  34.6 0.0 all-gather.3.cloned.1.call-update
  34.7 60.6 %all_to_all.25.refs_2_ = bf16[16,8,6,24,128]{4,3,2,1,0:T(8,128)(2,1)} all-to-all(bf16[16,8,6,24,128]{4,3,2,1,0:T(8,128)(2,1)} %shard_map.73), channel_id=1, replica_groups=mesh['sect'=16,'rup'=8] {'sect'}, dimensions={0} | all-to-all | bytes 9437184 | tf_op jit(solution)/shard_map/all_to_all | solution.py:282
  95.3 0.0 all-gather.3.cloned.1.call-done
  95.3 84.6 %all_to_all.26 = bf16[128,6,2,16,128]{4,3,2,1,0:T(8,128)(2,1)} all-to-all(bf16[128,6,2,16,128]{4,3,2,1,0:T(8,128)(2,1)} %bitcast.19), channel_id=1, replica_groups=mesh['sect'=16,'rup'=8] {'sect','rup'}, dimensions={0} | all-to-all | bytes 12582912 | tf_op jit(solution)/shard_map/all_to_all | solution.py:295
  179.9 6.1 %all-to-all-start.3 = ((bf16[128,2,2,16,128]{4,3,2,1,0:T(8,128)(2,1)}), bf16[128,2,2,16,128]{4,3,2,1,0:T(8,128)(2,1)S(1)}, u32[]{:S(2)}, u32[]{:S(2)}) async-start(bf16[128,2,2,16,128]{4,3,2,1,0:T(8,128)(2,1)} %bitcast.8), calls=%async_computation.3 | async-start | bytes 4194304 | tf_op jit(solution)/shard_map/all_to_all | solution.py:295
  186.0 25.7 %shard_map.75.refs_4_ = f32[64,128]{1,0:T(8,128)} custom-call(bf16[16,8,6,2,16,128]{5,4,3,2,1,0:T(8,128)(2,1)} %bitcast.20, bf16[8,16,7,16,128]{4,3,2,1,0:T(8,128)(2,1)} %bitcast.24, bf16[16,8,6,24,128]{4,3,2,1,0:T(8,128)(2,1)} %all_to_all.25.refs_2_, bf16[2,384,128]{2,1,0:T(8,128)(2,1)} %constant.40.clone.refs_3_), custom_call_target="tpu_custom_call" | custom-call | flops 14495514624 | bytes 9830400 | tf_op jit(solution)/shard_map/pallas_call | solution.py:174
  211.7 4.7 %all-to-all-done.3 = bf16[128,2,2,16,128]{4,3,2,1,0:T(8,128)(2,1)S(1)} async-done(((bf16[128,2,2,16,128]{4,3,2,1,0:T(8,128)(2,1)}), bf16[128,2,2,16,128]{4,3,2,1,0:T(8,128)(2,1)S(1)}, u32[]{:S(2)}, u32[]{:S(2)}) %all-to-all-start.3) | async-done | bytes 2097184 | tf_op jit(solution)/shard_map/all_to_all | solution.py:295
  216.4 0.0 copy-start
  216.4 1.3 copy-done
  217.7 0.0 copy-start.2
  217.7 10.9 %shard_map.76 = f32[128,4,128]{2,1,0:T(4,128)} custom-call(bf16[16,8,2,2,16,128]{5,4,3,2,1,0:T(8,128)(2,1)} %bitcast.22, bf16[8,16,7,16,128]{4,3,2,1,0:T(8,128)(2,1)} %bitcast.25, bf16[16,8,6,24,128]{4,3,2,1,0:T(8,128)(2,1)} %all_to_all.25.refs_2_, bf16[2,384,128]{2,1,0:T(8,128)(2,1)} %constant.40.clone.refs_3_, f32[64,128]{1,0:T(8,128)} %shard_map.75.refs_4_), custom_call_target="tpu_custom_call" | custom-call | flops 4831838208 | bytes 3276800 | tf_op jit(solution)/shard_map/pallas_call | solution.py:174
  228.6 0.1 fusion.12
  228.7 0.0 copy-done.2
  228.7 0.6 fusion.4
  229.3 5.1 %all-to-all-start.4 = ((f32[128,4,128]{2,1,0:T(4,128)}), f32[128,4,128]{2,1,0:T(4,128)S(1)}, u32[]{:S(2)}, u32[]{:S(2)}) async-start(f32[128,4,128]{2,1,0:T(4,128)} %shard_map.76), calls=%async_computation.4 | async-start | bytes 524288 | tf_op jit(solution)/shard_map/all_to_all | solution.py:307
  234.3 0.3 multiply_subtract_fusion
  234.6 0.2 maximum_multiply_fusion
  234.8 0.4 fusion
  235.1 10.0 %all-to-all-done.4.spectra_ref = f32[128,4,128]{2,1,0:T(4,128)S(1)} async-done(((f32[128,4,128]{2,1,0:T(4,128)}), f32[128,4,128]{2,1,0:T(4,128)S(1)}, u32[]{:S(2)}, u32[]{:S(2)}) %all-to-all-start.4) | async-done | bytes 262176 | tf_op jit(solution)/shard_map/all_to_all | solution.py:307
  245.1 1.2 shard_map.77
  (2 shorter events, 0.0 us)
Async XLA Ops:
  9.0 24.9 %all-to-all-start = ((bf16[16,7,16,128]{3,2,1,0:T(8,128)(2,1)}), bf16[16,7,16,128]{3,2,1,0:T(8,128)(2,1)S(1)}, u32[]{:S(2)}, u32[]{:S(2)}) async-start(bf16[16,7,16,128]{3,2,1,0:T(8,128)(2,1)} %broadcast_in_dim.8), calls=%async_computation | async-start | bytes 917504 | tf_op jit(solution)/shard_map/all_to_all | solution.py:276
  17.4 77.9 %all-gather.3.cloned.1.call-start = ((), (), s32[]{:S(2)}) async-start(), calls=%async_computation.5 | async-start | bytes 4128768 | tf_op jit(solution)/shard_map/all_gather | solution.py:281
  33.9 0.8 copy-start.1
  179.9 36.5 %all-to-all-start.3 = ((bf16[128,2,2,16,128]{4,3,2,1,0:T(8,128)(2,1)}), bf16[128,2,2,16,128]{4,3,2,1,0:T(8,128)(2,1)S(1)}, u32[]{:S(2)}, u32[]{:S(2)}) async-start(bf16[128,2,2,16,128]{4,3,2,1,0:T(8,128)(2,1)} %bitcast.8), calls=%async_computation.3 | async-start | bytes 4194304 | tf_op jit(solution)/shard_map/all_to_all | solution.py:295
  216.4 1.3 copy-start
  217.7 10.9 %copy-start.2 = (s32[128]{0:T(128)S(1)}, s32[128]{0:T(128)}, u32[]{:S(2)}) copy-start(s32[128]{0:T(128)} %constant.41.clone) | copy-start | bytes 1540
  229.3 15.8 %all-to-all-start.4 = ((f32[128,4,128]{2,1,0:T(4,128)}), f32[128,4,128]{2,1,0:T(4,128)S(1)}, u32[]{:S(2)}, u32[]{:S(2)}) async-start(f32[128,4,128]{2,1,0:T(4,128)} %shard_map.76), calls=%async_computation.4 | async-start | bytes 524288 | tf_op jit(solution)/shard_map/all_to_all | solution.py:307
Sparse Core Ops, SparseCore 0:
  34.8 32.3 all-gather.2

commit v3 on v2

--- a/solution.py
+++ b/solution.py
@@ -21,67 +21,107 @@
     return (jnp.cos(angles), jnp.sin(angles))
 
 
-def load_rows(in_ref, wide_ref):
-    rows = in_ref.shape[0]
+def load_rows(block_ref, wide_ref):
+    rows = block_ref.shape[0]
     apart = wide_ref.shape[0] // rows
     for r in range(rows):
-        block = in_ref[r].astype(jnp.float32).reshape(-1, in_ref.shape[-1])
+        block = block_ref[r].astype(jnp.float32).reshape(-1, block_ref.shape[-1])
         wide_ref[pl.ds(r * apart, block.shape[0])] = block
     return rows, apart
 
 
-def split_slip_kernel(slip_ref, *refs):
-    out_refs, wide_ref = refs[:-1], refs[-1]
-    rows, apart = load_rows(slip_ref, wide_ref)
-    lists, parts, devices, sub = slip_ref.shape[1:5]
-    for part in range(parts):
-        for d in range(devices):
-            f = 0
-            for out_ref in out_refs:
-                for i in range(out_ref.shape[2]):
-                    places = [((l * parts + part) * devices + d) * sub + f for l in range(lists)]
-                    turned = [wide_ref[pl.ds(place, rows, stride=apart)] for place in places]
-                    out_ref[d, 0, i, part] = jnp.concatenate(turned, axis=0).astype(slip_ref.dtype)
-                    f += 1
-
-
-def split_slip(slip, counts, sects):
-    rows, lists, parts, devices, sub, points = slip.shape
-    shapes = [(sects, devices // sects, count, parts, lists * rows, points) for count in counts]
+def split_kernel(count, *refs):
+    green_ref, slip_ref, green_out = refs[:3]
+    slip_outs = refs[3 : 3 + count]
+    green_in, slip_in, green_stage = refs[3 + count : 6 + count]
+    slip_stages = refs[6 + count : 6 + 2 * count]
+    green_wide, slip_wide, green_got, green_sent, slip_got, slip_sent = refs[6 + 2 * count :]
+    comps, _, dirs, sects, sub, _ = green_in.shape
+    rups, _, lists, parts = slip_in.shape[:4]
+
+    def green_load(c):
+        return pltpu.make_async_copy(green_ref.at[:, c], green_in.at[c], green_got.at[c])
+
+    def slip_load(k):
+        piece = slip_ref.at[:, :, :, pl.ds(k * sects, sects)]
+        return pltpu.make_async_copy(piece, slip_in.at[k], slip_got.at[k])
+
+    def green_store():
+        return pltpu.make_async_copy(green_stage, green_out, green_sent)
+
+    def slip_store(i, k):
+        return pltpu.make_async_copy(slip_stages[i].at[:, k], slip_outs[i].at[:, k], slip_sent.at[i, k])
+
+    for c in range(comps):
+        green_load(c).start()
+    for k in range(rups):
+        slip_load(k).start()
+
+    def green_step(c, carry):
+        green_load(c).wait()
+        rows, apart = load_rows(green_in.at[c], green_wide)
+        for s in range(sects):
+            for f in range(sub):
+                places = [(j * sects + s) * sub + f for j in range(dirs)]
+                turned = [green_wide[pl.ds(place, rows, stride=apart)] for place in places]
+                green_stage[s, f, c] = jnp.concatenate(turned, axis=0).astype(green_stage.dtype)
+        return carry
+
+    lax.fori_loop(0, comps, green_step, 0)
+    green_store().start()
+
+    def slip_step(k, carry):
+        slip_load(k).wait()
+        rows, apart = load_rows(slip_in.at[k], slip_wide)
+        for part in range(parts):
+            for d in range(sects):
+                f = 0
+                for stage in slip_stages:
+                    for i in range(stage.shape[2]):
+                        places = [((l * parts + part) * sects + d) * sub + f for l in range(lists)]
+                        turned = [slip_wide[pl.ds(place, rows, stride=apart)] for place in places]
+                        stage[d, k, i, part] = jnp.concatenate(turned, axis=0).astype(stage.dtype)
+                        f += 1
+        for i in range(count):
+            slip_store(i, k).start()
+        return carry
+
+    lax.fori_loop(0, rups, slip_step, 0)
+    green_store().wait()
+    for k in range(rups):
+        for i in range(count):
+            slip_store(i, k).wait()
+
+
+def split(green, slip, counts):
+    green_rows, comps, dirs, sects, sub, points = green.shape
+    rows, lists, parts, devices = slip.shape[:4]
+    rups = devices // sects
+    green_shape = (sects, sub, comps, dirs * green_rows, points)
+    slip_shapes = [(sects, rups, count, parts, lists * rows, points) for count in counts]
+    kind = green.dtype
+    anywhere = pl.BlockSpec(memory_space=pl.ANY)
     return pl.pallas_call(
-        split_slip_kernel,
-        grid=(devices // sects,),
-        in_specs=[pl.BlockSpec((rows, lists, parts, sects, sub, points), lambda k: (0, 0, 0, k, 0, 0))],
-        out_specs=[pl.BlockSpec((sects, 1) + shape[2:], lambda k: (0, k, 0, 0, 0, 0)) for shape in shapes],
-        out_shape=[jax.ShapeDtypeStruct(shape, slip.dtype) for shape in shapes],
-        scratch_shapes=[pltpu.VMEM((rows * (lists * parts * sects * sub + PAD), points), jnp.float32)],
+        functools.partial(split_kernel, len(counts)),
+        in_specs=[anywhere, anywhere],
+        out_specs=[anywhere] * (1 + len(counts)),
+        out_shape=[jax.ShapeDtypeStruct(shape, kind) for shape in [green_shape] + slip_shapes],
+        scratch_shapes=[
+            pltpu.VMEM((comps, green_rows, dirs, sects, sub, points), kind),
+            pltpu.VMEM((rups, rows, lists, parts, sects, sub, points), kind),
+            *[pltpu.VMEM(shape, kind) for shape in [green_shape] + slip_shapes],
+            pltpu.VMEM((green_rows * (dirs * sects * sub + PAD), points), jnp.float32),
+            pltpu.VMEM((rows * (lists * parts * sects * sub + PAD), points), jnp.float32),
+            pltpu.SemaphoreType.DMA((comps,)),
+            pltpu.SemaphoreType.DMA,
+            pltpu.SemaphoreType.DMA((rups,)),
+            pltpu.SemaphoreType.DMA((len(counts), rups)),
+        ],
         compiler_params=pltpu.CompilerParams(vmem_limit_bytes=60 * 2**20),
-    )(slip)
-
-
-def split_green_kernel(green_ref, out_ref, wide_ref):
-    rows, apart = load_rows(green_ref, wide_ref)
-    comps, dirs, sects, sub = green_ref.shape[1:5]
-    for s in range(sects):
-        for c in range(comps):
-            for f in range(sub):
-                places = [((c * dirs + j) * sects + s) * sub + f for j in range(dirs)]
-                turned = [wide_ref[pl.ds(place, rows, stride=apart)] for place in places]
-                out_ref[s, f, c] = jnp.concatenate(turned, axis=0).astype(green_ref.dtype)
-
-
-def split_green(green, sects):
-    rows, comps, dirs, _, sub, points = green.shape
-    shape = (sects, sub, comps, dirs * rows, points)
-    return pl.pallas_call(
-        split_green_kernel,
-        grid=(comps,),
-        in_specs=[pl.BlockSpec((rows, 1, dirs, sects, sub, points), lambda c: (0, c, 0, 0, 0, 0))],
-        out_specs=pl.BlockSpec((sects, sub, 1) + shape[3:], lambda c: (0, 0, c, 0, 0)),
-        out_shape=jax.ShapeDtypeStruct(shape, green.dtype),
-        scratch_shapes=[pltpu.VMEM((rows * (dirs * sects * sub + PAD), points), jnp.float32)],
-        compiler_params=pltpu.CompilerParams(vmem_limit_bytes=60 * 2**20),
-    )(green)
+        cost_estimate=pl.CostEstimate(
+            flops=2 * (green.size + slip.size), bytes_accessed=4 * (green.size + slip.size), transcendentals=0
+        ),
+    )(green, slip)
 
 
 def contract_kernel(width, blocks, sub, first, final, *refs):
@@ -178,7 +218,7 @@
         out_specs=pl.BlockSpec(shape, lambda f: (0,) * len(shape)),
         out_shape=jax.ShapeDtypeStruct(shape, jnp.float32),
         scratch_shapes=scratch,
-        compiler_params=pltpu.CompilerParams(vmem_limit_bytes=60 * 2**20),
+        compiler_params=pltpu.CompilerParams(vmem_limit_bytes=63_400_000),
         cost_estimate=pl.CostEstimate(
             flops=freqs * 4 * sects * rups * entries * comps * points * cols,
             bytes_accessed=freqs * (sects * rups * entries * points * 4 + comps * cols * points * 2),
@@ -275,8 +315,11 @@
     moment, green_tensor, slip_rate = lax.optimization_barrier((moment, green_tensor, slip_rate))
     moment = lax.all_to_all(moment, "sect", split_axis=0, concat_axis=0, tiled=True)
 
-    green = split_green(green_tensor.reshape(blocks * 2, comps, dirs, sects, sub, points), sects)
-    parts = split_slip(slip_rate.reshape(rup_rows, list_cols, 2, rups * sects, sub, points), PARTS, sects)
+    green, *parts = split(
+        green_tensor.reshape(blocks * 2, comps, dirs, sects, sub, points),
+        slip_rate.reshape(rup_rows, list_cols, 2, rups * sects, sub, points),
+        PARTS,
+    )
     green, moment, *parts = lax.optimization_barrier((green, moment, *parts))
     moment = lax.all_gather(moment, "rup", axis=0)
     green = lax.all_to_all(green, "sect", split_axis=0, concat_axis=0, tiled=True)

time: 254 us -> 247 us (0.972)
  Pallas kernels: 54.1 us -> 47.5 us
    pallas_call x2 -> x1, Pallas kernels: 16.4 us -> 9.77 us  [split(): pl.pallas_call(functools.partial(split_kernel, len(counts)), in_specs=[an...]
  transfers between devices with their start and end apart: 4 -> 4, of which waited for: 2 -> 2; matrix products, arithmetic and copies ran while one was open for 0% -> 0% of each run, Pallas kernels for 17% -> 14%
where the time goes in v3:
time: 247 us
  blocking collectives  145 us (59%)
  Pallas kernels  47.5 us (19%)
  starting transfers between devices  19.7 us (8%)
  waiting for transfers between devices  14.7 us (6%)
  between operations  13.5 us (5%)
  local copies, waits for them, and re-layouts  3.84 us (2%)
    all_to_all x1, blocking collectives, body(): lax.all_to_all(arrived, both, split_axis=0, concat_axis=0, tiled=True)  84.6 us
    all_to_all x1, blocking collectives, body(): lax.all_to_all(green, 'sect', split_axis=0, concat_axis=0, tiled=True)  60.6 us
    pallas_call x2, Pallas kernels, contract(): pl.pallas_call(functools.partial(contract_kernel, width, blocks, sub, fir...  36.5 us
    all_to_all x1, waiting for transfers between devices, body(): lax.all_to_all(send, both, split_axis=0, concat_axis=0, tiled=True)  9.97 us
    pallas_call x1, Pallas kernels, split(): pl.pallas_call(functools.partial(split_kernel, len(counts)), in_specs=[an...  9.77 us
    all_to_all x1, starting transfers between devices, body(): lax.all_to_all(moment, 'sect', split_axis=0, concat_axis=0, tiled=True)  8.43 us
    all_to_all x1, starting transfers between devices, body(): lax.all_to_all(arrived, both, split_axis=0, concat_axis=0, tiled=True)  6.15 us
    all_to_all x1, starting transfers between devices, body(): lax.all_to_all(send, both, split_axis=0, concat_axis=0, tiled=True)  5.05 us
  transfers between devices with their start and end apart: 4, of which 2 were waited for; matrix products, arithmetic and copies ran while one was open for 0% of the time, Pallas kernels for 14%

profile of v3, /device:TPU:1, one launch (start us, length us, event | category | flops | bytes accessed | tf_op | source)
XLA Modules:
  0.0 246.5 jit_solution(11503222666065496025)
XLA Ops:
  6.5 0.7 copy.11
  7.3 0.7 fusion.14
  8.0 0.1 broadcast_in_dim.6
  8.1 0.1 broadcast_in_dim.7
  8.1 0.8 broadcast_in_dim.8
  9.0 8.4 %all-to-all-start = ((bf16[16,7,16,128]{3,2,1,0:T(8,128)(2,1)}), bf16[16,7,16,128]{3,2,1,0:T(8,128)(2,1)S(1)}, u32[]{:S(2)}, u32[]{:S(2)}) async-start(bf16[16,7,16,128]{3,2,1,0:T(8,128)(2,1)} %broadcast_in_dim.8), calls=%async_computation | async-start | bytes 917504 | tf_op jit(solution)/shard_map/all_to_all | solution.py:316
  17.4 0.0 all-gather.3.cloned.1.call-start
  17.5 9.8 %shard_map.73 = (bf16[16,8,6,24,128]{4,3,2,1,0:T(8,128)(2,1)}, bf16[16,8,6,2,16,128]{5,4,3,2,1,0:T(8,128)(2,1)}, bf16[16,8,2,2,16,128]{5,4,3,2,1,0:T(8,128)(2,1)}) custom-call(bf16[8,6,3,16,8,128]{5,4,3,2,1,0:T(8,128)(2,1)} %bitcast.21, bf16[8,2,2,128,8,128]{5,4,3,2,1,0:T(8,128)(2,1)} %bitcast.18), custom_call_target="tpu_custom_call" | custom-call | flops 13107200 | bytes 26214400 | tf_op jit(solution)/shard_map/pallas_call | solution.py:104
  27.2 0.0 all-to-all-done
  27.3 0.0 copy-start.1
  27.3 0.8 copy-done.1
  28.0 0.0 all-gather.3.cloned.1.call-update
  28.1 60.6 %all_to_all.25.refs_2_ = bf16[16,8,6,24,128]{4,3,2,1,0:T(8,128)(2,1)} all-to-all(bf16[16,8,6,24,128]{4,3,2,1,0:T(8,128)(2,1)} %get-tuple-element.34), channel_id=1, replica_groups=mesh['sect'=16,'rup'=8] {'sect'}, dimensions={0} | all-to-all | bytes 9437184 | tf_op jit(solution)/shard_map/all_to_all | solution.py:325
  88.7 0.0 all-gather.3.cloned.1.call-done
  88.7 84.6 %all_to_all.26 = bf16[128,6,2,16,128]{4,3,2,1,0:T(8,128)(2,1)} all-to-all(bf16[128,6,2,16,128]{4,3,2,1,0:T(8,128)(2,1)} %bitcast.19), channel_id=1, replica_groups=mesh['sect'=16,'rup'=8] {'sect','rup'}, dimensions={0} | all-to-all | bytes 12582912 | tf_op jit(solution)/shard_map/all_to_all | solution.py:338
  173.3 6.1 %all-to-all-start.3 = ((bf16[128,2,2,16,128]{4,3,2,1,0:T(8,128)(2,1)}), bf16[128,2,2,16,128]{4,3,2,1,0:T(8,128)(2,1)S(1)}, u32[]{:S(2)}, u32[]{:S(2)}) async-start(bf16[128,2,2,16,128]{4,3,2,1,0:T(8,128)(2,1)} %bitcast.8), calls=%async_computation.3 | async-start | bytes 4194304 | tf_op jit(solution)/shard_map/all_to_all | solution.py:338
  179.4 25.7 %shard_map.74.refs_4_ = f32[64,128]{1,0:T(8,128)} custom-call(bf16[16,8,6,2,16,128]{5,4,3,2,1,0:T(8,128)(2,1)} %bitcast.20, bf16[8,16,7,16,128]{4,3,2,1,0:T(8,128)(2,1)} %bitcast.24, bf16[16,8,6,24,128]{4,3,2,1,0:T(8,128)(2,1)} %all_to_all.25.refs_2_, bf16[2,384,128]{2,1,0:T(8,128)(2,1)} %constant.40.clone.refs_3_), custom_call_target="tpu_custom_call" | custom-call | flops 14495514624 | bytes 9830400 | tf_op jit(solution)/shard_map/pallas_call | solution.py:214
  205.1 4.7 %all-to-all-done.3 = bf16[128,2,2,16,128]{4,3,2,1,0:T(8,128)(2,1)S(1)} async-done(((bf16[128,2,2,16,128]{4,3,2,1,0:T(8,128)(2,1)}), bf16[128,2,2,16,128]{4,3,2,1,0:T(8,128)(2,1)S(1)}, u32[]{:S(2)}, u32[]{:S(2)}) %all-to-all-start.3) | async-done | bytes 2097184 | tf_op jit(solution)/shard_map/all_to_all | solution.py:338
  209.8 0.0 copy-start
  209.8 1.3 copy-done
  211.1 0.0 copy-start.2
  211.1 10.9 %shard_map.75 = f32[128,4,128]{2,1,0:T(4,128)} custom-call(bf16[16,8,2,2,16,128]{5,4,3,2,1,0:T(8,128)(2,1)} %bitcast.22, bf16[8,16,7,16,128]{4,3,2,1,0:T(8,128)(2,1)} %bitcast.25, bf16[16,8,6,24,128]{4,3,2,1,0:T(8,128)(2,1)} %all_to_all.25.refs_2_, bf16[2,384,128]{2,1,0:T(8,128)(2,1)} %constant.40.clone.refs_3_, f32[64,128]{1,0:T(8,128)} %shard_map.74.refs_4_), custom_call_target="tpu_custom_call" | custom-call | flops 4831838208 | bytes 3276800 | tf_op jit(solution)/shard_map/pallas_call | solution.py:214
  222.0 0.1 fusion.12
  222.1 0.0 copy-done.2
  222.1 0.6 fusion.4
  222.7 5.1 %all-to-all-start.4 = ((f32[128,4,128]{2,1,0:T(4,128)}), f32[128,4,128]{2,1,0:T(4,128)S(1)}, u32[]{:S(2)}, u32[]{:S(2)}) async-start(f32[128,4,128]{2,1,0:T(4,128)} %shard_map.75), calls=%async_computation.4 | async-start | bytes 524288 | tf_op jit(solution)/shard_map/all_to_all | solution.py:350
  227.7 0.3 multiply_subtract_fusion
  228.0 0.2 maximum_multiply_fusion
  228.2 0.4 fusion
  228.5 10.0 %all-to-all-done.4.spectra_ref = f32[128,4,128]{2,1,0:T(4,128)S(1)} async-done(((f32[128,4,128]{2,1,0:T(4,128)}), f32[128,4,128]{2,1,0:T(4,128)S(1)}, u32[]{:S(2)}, u32[]{:S(2)}) %all-to-all-start.4) | async-done | bytes 262176 | tf_op jit(solution)/shard_map/all_to_all | solution.py:350
  238.5 1.2 shard_map.76
  (2 shorter events, 0.0 us)
Async XLA Ops:
  9.0 18.3 %all-to-all-start = ((bf16[16,7,16,128]{3,2,1,0:T(8,128)(2,1)}), bf16[16,7,16,128]{3,2,1,0:T(8,128)(2,1)S(1)}, u32[]{:S(2)}, u32[]{:S(2)}) async-start(bf16[16,7,16,128]{3,2,1,0:T(8,128)(2,1)} %broadcast_in_dim.8), calls=%async_computation | async-start | bytes 917504 | tf_op jit(solution)/shard_map/all_to_all | solution.py:316
  17.4 71.3 %all-gather.3.cloned.1.call-start = ((), (), s32[]{:S(2)}) async-start(), calls=%async_computation.5 | async-start | bytes 4128768 | tf_op jit(solution)/shard_map/all_gather | solution.py:324
  27.3 0.8 copy-start.1
  173.3 36.5 %all-to-all-start.3 = ((bf16[128,2,2,16,128]{4,3,2,1,0:T(8,128)(2,1)}), bf16[128,2,2,16,128]{4,3,2,1,0:T(8,128)(2,1)S(1)}, u32[]{:S(2)}, u32[]{:S(2)}) async-start(bf16[128,2,2,16,128]{4,3,2,1,0:T(8,128)(2,1)} %bitcast.8), calls=%async_computation.3 | async-start | bytes 4194304 | tf_op jit(solution)/shard_map/all_to_all | solution.py:338
  209.8 1.3 copy-start
  211.1 10.9 %copy-start.2 = (s32[128]{0:T(128)S(1)}, s32[128]{0:T(128)}, u32[]{:S(2)}) copy-start(s32[128]{0:T(128)} %constant.41.clone) | copy-start | bytes 1540
  222.7 15.8 %all-to-all-start.4 = ((f32[128,4,128]{2,1,0:T(4,128)}), f32[128,4,128]{2,1,0:T(4,128)S(1)}, u32[]{:S(2)}, u32[]{:S(2)}) async-start(f32[128,4,128]{2,1,0:T(4,128)} %shard_map.75), calls=%async_computation.4 | async-start | bytes 524288 | tf_op jit(solution)/shard_map/all_to_all | solution.py:350
Sparse Core Ops, SparseCore 0:
  28.2 32.3 all-gather.2

commit v4 on v3

--- a/solution.py
+++ b/solution.py
@@ -13,12 +13,6 @@
 STEP = 16
 LANES = 128
 PAD = 1
-
-
-def phase_table(freq_ids, time_ids, samples):
-    phases = freq_ids[:, None] * time_ids[None, :] % samples
-    angles = phases.astype(jnp.float32) * (2.0 * math.pi / samples)
-    return (jnp.cos(angles), jnp.sin(angles))
 
 
 def load_rows(block_ref, wide_ref):
@@ -117,7 +111,7 @@
             pltpu.SemaphoreType.DMA((rups,)),
             pltpu.SemaphoreType.DMA((len(counts), rups)),
         ],
-        compiler_params=pltpu.CompilerParams(vmem_limit_bytes=60 * 2**20),
+        compiler_params=pltpu.CompilerParams(vmem_limit_bytes=67_000_000),
         cost_estimate=pl.CostEstimate(
             flops=2 * (green.size + slip.size), bytes_accessed=4 * (green.size + slip.size), transcendentals=0
         ),
@@ -218,7 +212,7 @@
         out_specs=pl.BlockSpec(shape, lambda f: (0,) * len(shape)),
         out_shape=jax.ShapeDtypeStruct(shape, jnp.float32),
         scratch_shapes=scratch,
-        compiler_params=pltpu.CompilerParams(vmem_limit_bytes=63_400_000),
+        compiler_params=pltpu.CompilerParams(vmem_limit_bytes=67_000_000),
         cost_estimate=pl.CostEstimate(
             flops=freqs * 4 * sects * rups * entries * comps * points * cols,
             bytes_accessed=freqs * (sects * rups * entries * points * 4 + comps * cols * points * 2),
@@ -240,17 +234,20 @@
     return jnp.asarray(np.stack([real_slip, imag_slip]), jnp.bfloat16)
 
 
-def transform_table(first_time, times, frequencies, sects, rups, sub):
+def transform_table(rup, times, frequencies, sects, rups, sub):
     samples = 2 * frequencies
-    time_ids = first_time + jnp.arange(times, dtype=jnp.int32)
+    unit = 2.0 * math.pi / samples
     base = np.arange(sects)[:, None] * sub + np.arange(rups)[None, :] * (frequencies // rups)
-    base_cos, base_sin = phase_table(jnp.asarray(base.reshape(-1), jnp.int32), time_ids, samples)
-    rest_cos, rest_sin = phase_table(jnp.arange(sub, dtype=jnp.int32), time_ids, samples)
-    base_cos, base_sin, rest_cos, rest_sin = lax.optimization_barrier((base_cos, base_sin, rest_cos, rest_sin))
+    base = base.reshape(-1, 1) * np.arange(times)[None, :] % samples * unit
+    rest = np.arange(sub)[None, :, None] * np.arange(samples).reshape(rups, 1, times) % samples * unit
+    scale = 1.0 / math.sqrt(frequencies)
+    base_cos, base_sin = (jnp.asarray(f(base) * scale, jnp.float32) for f in (np.cos, np.sin))
+    rest_cos, rest_sin = (
+        lax.dynamic_index_in_dim(jnp.asarray(f(rest), jnp.float32), rup, 0, keepdims=False) for f in (np.cos, np.sin)
+    )
     cosine = rest_cos[:, None] * base_cos[None] - rest_sin[:, None] * base_sin[None]
     sine = rest_sin[:, None] * base_cos[None] + rest_cos[:, None] * base_sin[None]
-    table = jnp.stack([cosine, -sine]) * (1.0 / math.sqrt(frequencies))
-    table = table.reshape(2 * frequencies, times)
+    table = jnp.stack([cosine, -sine]).reshape(2 * frequencies, times)
     high = lax.reduce_precision(table, 8, 7)
     return high.astype(jnp.bfloat16), (table - high).astype(jnp.bfloat16)
 
@@ -325,7 +322,7 @@
     green = lax.all_to_all(green, "sect", split_axis=0, concat_axis=0, tiled=True)
 
     fold = fold_table(cols, blocks, sub)
-    first_time = lax.axis_index("rup") * (2 * frequencies // rups)
+    rup = lax.axis_index("rup")
     spectrum = None
     first = 0
     before = green
@@ -344,8 +341,8 @@
         before = arrived.reshape(part.shape)
         first += part.shape[2]
     send = contract(before, moment, green, fold, spectrum, done, width, blocks)
-    first_time, send = lax.optimization_barrier((first_time, send))
-    high, low = transform_table(first_time, 2 * frequencies // rups, frequencies, sects, rups, sub)
+    rup, send = lax.optimization_barrier((rup, send))
+    high, low = transform_table(rup, 2 * frequencies // rups, frequencies, sects, rups, sub)
 
     all_freqs = lax.all_to_all(send, both, split_axis=0, concat_axis=0, tiled=True)
     return jnp.swapaxes(transform(all_freqs, high, low, dirs, sub), 0, 1)

time: 247 us -> 245 us (level)
  transfers between devices with their start and end apart: 4 -> 4, of which waited for: 2 -> 2; matrix products, arithmetic and copies ran while one was open for 0% -> 1% of each run, Pallas kernels for 14% -> 15%
where the time goes in v4:
time: 245 us; the launch traced here: 244 us
  blocking collectives  145 us (59%)
  Pallas kernels  47.5 us (19%)
  starting transfers between devices  20.5 us (8%)
  between operations  13.5 us (6%)
  waiting for transfers between devices  12.6 us (5%)
  other arithmetic  2.48 us (1%)
  local copies, waits for them, and re-layouts  2.45 us (1%)
    all_to_all x1, blocking collectives, body(): lax.all_to_all(arrived, both, split_axis=0, concat_axis=0, tiled=True)  84.6 us
    all_to_all x1, blocking collectives, body(): lax.all_to_all(green, 'sect', split_axis=0, concat_axis=0, tiled=True)  60.6 us
    pallas_call x2, Pallas kernels, contract(): pl.pallas_call(functools.partial(contract_kernel, width, blocks, sub, fir...  36.5 us
    pallas_call x1, Pallas kernels, split(): pl.pallas_call(functools.partial(split_kernel, len(counts)), in_specs=[an...  9.77 us
    all_to_all x1, starting transfers between devices, body(): lax.all_to_all(moment, 'sect', split_axis=0, concat_axis=0, tiled=True)  8.47 us
    all_to_all x1, waiting for transfers between devices, body(): lax.all_to_all(send, both, split_axis=0, concat_axis=0, tiled=True)  8.26 us
    all_to_all x1, starting transfers between devices, body(): lax.all_to_all(arrived, both, split_axis=0, concat_axis=0, tiled=True)  6.61 us
    all_to_all x1, starting transfers between devices, body(): lax.all_to_all(send, both, split_axis=0, concat_axis=0, tiled=True)  5.43 us
  transfers between devices with their start and end apart: 4, of which 2 were waited for; matrix products, arithmetic and copies ran while one was open for 1% of the time, Pallas kernels for 15%

profile of v4, /device:TPU:1, one launch (start us, length us, event | category | flops | bytes accessed | tf_op | source)
XLA Modules:
  0.0 244.2 jit_solution(14199744616741244525)
XLA Ops:
  6.5 0.7 copy.14
  7.3 0.7 fusion.1
  8.0 0.1 broadcast_in_dim.6
  8.1 0.1 broadcast_in_dim.7
  8.1 0.8 broadcast_in_dim.8
  9.0 8.5 %all-to-all-start = ((bf16[16,7,16,128]{3,2,1,0:T(8,128)(2,1)}), bf16[16,7,16,128]{3,2,1,0:T(8,128)(2,1)}, u32[]{:S(2)}, u32[]{:S(2)}) async-start(bf16[16,7,16,128]{3,2,1,0:T(8,128)(2,1)} %broadcast_in_dim.8), calls=%async_computation | async-start | bytes 917504 | tf_op jit(solution)/shard_map/all_to_all | solution.py:313
  17.5 0.0 all-gather.3.cloned.1.call-start
  17.5 9.8 %shard_map.100 = (bf16[16,8,6,24,128]{4,3,2,1,0:T(8,128)(2,1)}, bf16[16,8,6,2,16,128]{5,4,3,2,1,0:T(8,128)(2,1)}, bf16[16,8,2,2,16,128]{5,4,3,2,1,0:T(8,128)(2,1)}) custom-call(bf16[8,6,3,16,8,128]{5,4,3,2,1,0:T(8,128)(2,1)} %bitcast.25, bf16[8,2,2,128,8,128]{5,4,3,2,1,0:T(8,128)(2,1)} %bitcast.22), custom_call_target="tpu_custom_call" | custom-call | flops 13107200 | bytes 26214400 | tf_op jit(solution)/shard_map/pallas_call | solution.py:98
  27.3 0.0 all-to-all-done
  27.3 0.0 all-gather.3.cloned.1.call-update
  27.3 60.6 %all_to_all.25.refs_2_ = bf16[16,8,6,24,128]{4,3,2,1,0:T(8,128)(2,1)} all-to-all(bf16[16,8,6,24,128]{4,3,2,1,0:T(8,128)(2,1)} %get-tuple-element.30), channel_id=1, replica_groups=mesh['sect'=16,'rup'=8] {'sect'}, dimensions={0} | all-to-all | bytes 9437184 | tf_op jit(solution)/shard_map/all_to_all | solution.py:322
  87.9 0.0 all-gather.3.cloned.1.call-done
  87.9 84.6 %all_to_all.26 = bf16[128,6,2,16,128]{4,3,2,1,0:T(8,128)(2,1)} all-to-all(bf16[128,6,2,16,128]{4,3,2,1,0:T(8,128)(2,1)} %bitcast.23), channel_id=1, replica_groups=mesh['sect'=16,'rup'=8] {'sect','rup'}, dimensions={0} | all-to-all | bytes 12582912 | tf_op jit(solution)/shard_map/all_to_all | solution.py:335
  172.5 6.6 %all-to-all-start.3 = ((bf16[128,2,2,16,128]{4,3,2,1,0:T(8,128)(2,1)}), bf16[128,2,2,16,128]{4,3,2,1,0:T(8,128)(2,1)}, u32[]{:S(2)}, u32[]{:S(2)}) async-start(bf16[128,2,2,16,128]{4,3,2,1,0:T(8,128)(2,1)} %bitcast.8), calls=%async_computation.3 | async-start | bytes 4194304 | tf_op jit(solution)/shard_map/all_to_all | solution.py:335
  179.1 25.7 %shard_map.101.refs_4_ = f32[64,128]{1,0:T(8,128)} custom-call(bf16[16,8,6,2,16,128]{5,4,3,2,1,0:T(8,128)(2,1)} %bitcast.24, bf16[8,16,7,16,128]{4,3,2,1,0:T(8,128)(2,1)} %bitcast.27, bf16[16,8,6,24,128]{4,3,2,1,0:T(8,128)(2,1)} %all_to_all.25.refs_2_, bf16[2,384,128]{2,1,0:T(8,128)(2,1)} %constant.24.clone.refs_3_), custom_call_target="tpu_custom_call" | custom-call | flops 14495514624 | bytes 9830400 | tf_op jit(solution)/shard_map/pallas_call | solution.py:208
  204.8 4.4 %all-to-all-done.3 = bf16[128,2,2,16,128]{4,3,2,1,0:T(8,128)(2,1)} async-done(((bf16[128,2,2,16,128]{4,3,2,1,0:T(8,128)(2,1)}), bf16[128,2,2,16,128]{4,3,2,1,0:T(8,128)(2,1)}, u32[]{:S(2)}, u32[]{:S(2)}) %all-to-all-start.3) | async-done | bytes 2097184 | tf_op jit(solution)/shard_map/all_to_all | solution.py:335
  209.1 10.8 %shard_map.102 = f32[128,4,128]{2,1,0:T(4,128)} custom-call(bf16[16,8,2,2,16,128]{5,4,3,2,1,0:T(8,128)(2,1)} %bitcast.9.refs_0_, bf16[8,16,7,16,128]{4,3,2,1,0:T(8,128)(2,1)} %bitcast.28, bf16[16,8,6,24,128]{4,3,2,1,0:T(8,128)(2,1)} %all_to_all.25.refs_2_, bf16[2,384,128]{2,1,0:T(8,128)(2,1)} %constant.24.clone.refs_3_, f32[64,128]{1,0:T(8,128)} %shard_map.101.refs_4_), custom_call_target="tpu_custom_call" | custom-call | flops 4831838208 | bytes 3276800 | tf_op jit(solution)/shard_map/pallas_call | solution.py:208
  219.9 5.4 %all-to-all-start.4 = ((f32[128,4,128]{2,1,0:T(4,128)}), f32[128,4,128]{2,1,0:T(4,128)S(1)}, u32[]{:S(2)}, u32[]{:S(2)}) async-start(f32[128,4,128]{2,1,0:T(4,128)} %shard_map.102), calls=%async_computation.4 | async-start | bytes 524288 | tf_op jit(solution)/shard_map/all_to_all | solution.py:347
  225.4 0.7 dynamic-slice_bitcast_fusion
  226.1 1.2 multiply_subtract_fusion
  227.3 0.2 pad_maximum_fusion
  227.5 0.4 fusion
  227.9 8.3 %all-to-all-done.4.spectra_ref = f32[128,4,128]{2,1,0:T(4,128)S(1)} async-done(((f32[128,4,128]{2,1,0:T(4,128)}), f32[128,4,128]{2,1,0:T(4,128)S(1)}, u32[]{:S(2)}, u32[]{:S(2)}) %all-to-all-start.4) | async-done | bytes 262176 | tf_op jit(solution)/shard_map/all_to_all | solution.py:347
  236.2 1.2 shard_map.103
  (1 shorter events, 0.0 us)
Async XLA Ops:
  9.0 18.3 %all-to-all-start = ((bf16[16,7,16,128]{3,2,1,0:T(8,128)(2,1)}), bf16[16,7,16,128]{3,2,1,0:T(8,128)(2,1)}, u32[]{:S(2)}, u32[]{:S(2)}) async-start(bf16[16,7,16,128]{3,2,1,0:T(8,128)(2,1)} %broadcast_in_dim.8), calls=%async_computation | async-start | bytes 917504 | tf_op jit(solution)/shard_map/all_to_all | solution.py:313
  17.5 70.4 %all-gather.3.cloned.1.call-start = ((), (), s32[]{:S(2)}) async-start(), calls=%async_computation.5 | async-start | bytes 4128768 | tf_op jit(solution)/shard_map/all_gather | solution.py:321
  172.5 36.7 %all-to-all-start.3 = ((bf16[128,2,2,16,128]{4,3,2,1,0:T(8,128)(2,1)}), bf16[128,2,2,16,128]{4,3,2,1,0:T(8,128)(2,1)}, u32[]{:S(2)}, u32[]{:S(2)}) async-start(bf16[128,2,2,16,128]{4,3,2,1,0:T(8,128)(2,1)} %bitcast.8), calls=%async_computation.3 | async-start | bytes 4194304 | tf_op jit(solution)/shard_map/all_to_all | solution.py:335
  219.9 16.2 %all-to-all-start.4 = ((f32[128,4,128]{2,1,0:T(4,128)}), f32[128,4,128]{2,1,0:T(4,128)S(1)}, u32[]{:S(2)}, u32[]{:S(2)}) async-start(f32[128,4,128]{2,1,0:T(4,128)} %shard_map.102), calls=%async_computation.4 | async-start | bytes 524288 | tf_op jit(solution)/shard_map/all_to_all | solution.py:347
Sparse Core Ops, SparseCore 0:
  27.4 32.3 all-gather.2

commit v5 on v4

--- a/solution.py
+++ b/solution.py
@@ -10,7 +10,6 @@
 from jax.sharding import PartitionSpec as P
 
 PARTS = (6, 2)
-STEP = 16
 LANES = 128
 PAD = 1
 
@@ -120,67 +119,56 @@
 
 def contract_kernel(width, blocks, sub, first, final, *refs):
     if final:
-        slip_ref, moment_ref, green_ref, fold_ref, prev_ref, out_ref, acc_ref, sum_ref = refs
+        slip_ref, moment_ref, green_ref, fold_ref, prev_ref, out_ref, sum_ref = refs
     else:
-        slip_ref, moment_ref, green_ref, fold_ref, sum_ref, acc_ref = refs
+        slip_ref, moment_ref, green_ref, fold_ref, sum_ref = refs
     rups, sects, rows_per = moment_ref.shape[:3]
     comps = rows_per - 1
     entries, points = moment_ref.shape[3:]
-    half = entries // 2
     cols = sects * width
     green = jnp.concatenate([green_ref[:, 0, c].reshape(cols, points) for c in range(comps)], axis=1)
-    col = lax.broadcasted_iota(jnp.int32, (1, 1, 1, cols), 3)
-    col_block = (col // width * blocks + col % (2 * blocks) // 2).astype(jnp.float32)
-    acc_ref[...] = jnp.zeros(acc_ref.shape, jnp.float32)
+    row = lax.broadcasted_iota(jnp.int32, (cols, LANES), 0)
+    row_block = (row // width * blocks + row % (2 * blocks) // 2).astype(jnp.float32)
+    ids = moment_ref[0, :, comps].astype(jnp.float32)
+    for k in range(1, rups):
+        ids = ids + moment_ref[k, :, comps].astype(jnp.float32)
     f = pl.program_id(0)
 
     @pl.when(f == 0)
     def _():
         sum_ref[...] = prev_ref[...] if final else jnp.zeros(sum_ref.shape, jnp.float32)
 
-    def step(i, carry):
-        some = pl.ds(i * STEP, STEP)
-        ids = moment_ref[:, some, comps].astype(jnp.float32)
-        mask = jnp.concatenate([ids] * (cols // points), axis=3) == col_block
-        for part in range(2):
-            slip = jnp.swapaxes(slip_ref[some, :, 0, part], 0, 1)
-            weighted = jnp.concatenate(
-                [
-                    (slip * moment_ref[:, some, c]).reshape(rups * STEP * entries, points)
-                    for c in range(comps)
-                ],
-                axis=1,
-            )
-            products = lax.dot_general(
-                weighted, green, (((1,), (1,)), ((), ())), preferred_element_type=jnp.float32
-            )
-            kept = jnp.where(mask, products.reshape(rups, STEP, entries, cols), 0.0)
-            kept = kept.reshape(rups, STEP, 2, half, cols)
-            total = kept[:, 0, 0] + kept[:, 0, 1]
-            for g in range(1, STEP):
-                total = total + kept[:, g, 0] + kept[:, g, 1]
-            acc_ref[part] += total
-        return carry
-
-    lax.fori_loop(0, sects // STEP, step, 0)
     spectrum = None
     for part in range(2):
-        rest = acc_ref[part].reshape(rups * half, cols)
+        slip = slip_ref[:, :, 0, part]
+        weighted = jnp.concatenate(
+            [
+                (slip * jnp.swapaxes(moment_ref[:, :, c], 0, 1)).reshape(sects * LANES, points)
+                for c in range(comps)
+            ],
+            axis=1,
+        )
+        products = lax.dot_general(green, weighted, (((1,), (1,)), ((), ())), preferred_element_type=jnp.float32)
+        rest = None
+        for s in range(sects):
+            kept = jnp.where(row_block == ids[s, :1], products[:, s * LANES : (s + 1) * LANES], 0.0)
+            rest = kept if rest is None else rest + kept
         for _ in range(3):
             piece = rest.astype(jnp.bfloat16)
-            term = jnp.dot(piece, fold_ref[part], preferred_element_type=jnp.float32)
+            term = jnp.dot(fold_ref[part], piece, preferred_element_type=jnp.float32)
             spectrum = term if spectrum is None else spectrum + term
             rest = rest - piece.astype(jnp.float32)
-    sum_ref[...] += pltpu.roll(spectrum, f + first, 1)
+    sum_ref[: spectrum.shape[0]] += pltpu.roll(spectrum, f + first, 0)
     if final:
 
         @pl.when(f == pl.num_programs(0) - 1)
         def _():
             owned = out_ref.shape[1]
+            turned = sum_ref[...].T.reshape(rups, 2, entries // 2, LANES)
+            turned = (turned[:, 0] + turned[:, 1]).reshape(rups * entries // 2, LANES)
             for s in range(sects):
-                mine = sum_ref[s * owned : (s + 1) * owned]
                 for k in range(rups):
-                    out_ref[s * rups + k] = mine
+                    out_ref[s * rups + k] = turned[s * owned : (s + 1) * owned]
 
 
 def contract(slip, moment, green, fold, prev, first, width, blocks):
@@ -197,14 +185,14 @@
         pl.BlockSpec(fold.shape, lambda f: (0, 0, 0)),
     ]
     args = [slip, moment, green, fold]
-    scratch = [pltpu.VMEM((2, rups, entries // 2, cols), jnp.float32)]
+    scratch = []
     if final:
         in_specs.append(pl.BlockSpec(prev.shape, lambda f: (0, 0)))
         args.append(prev)
         shape = (sects * rups, ruptures // sects, LANES)
-        scratch.append(pltpu.VMEM((ruptures, LANES), jnp.float32))
+        scratch.append(pltpu.VMEM((LANES, LANES), jnp.float32))
     else:
-        shape = (ruptures, LANES)
+        shape = (LANES, LANES)
     return pl.pallas_call(
         functools.partial(contract_kernel, width, blocks, sub, first, final),
         grid=(freqs,),
@@ -224,11 +212,11 @@
 def fold_table(cols, blocks, sub):
     col = np.arange(cols)
     part, direction = col % 2, col // (2 * blocks) % 3
-    out = np.arange(LANES)
-    value = np.where((out < 6 * sub) & (out % sub == 0), out // sub, -1)
-    same = (direction[:, None] == (value % 3)[None, :]) & (value >= 0)[None, :]
-    equal = part[:, None] == (value // 3)[None, :]
-    sign = np.where(value // 3 == 0, -1.0, 1.0)[None, :]
+    out = np.arange(6 * sub)
+    value = np.where(out % sub == 0, out // sub, -1)
+    same = (direction[None, :] == (value % 3)[:, None]) & (value >= 0)[:, None]
+    equal = part[None, :] == (value // 3)[:, None]
+    sign = np.where(value // 3 == 0, -1.0, 1.0)[:, None]
     real_slip = np.where(same & equal, 1.0, 0.0)
     imag_slip = np.where(same & ~equal, sign, 0.0)
     return jnp.asarray(np.stack([real_slip, imag_slip]), jnp.bfloat16)
@@ -304,8 +292,10 @@
     width = 2 * dirs * blocks
     cols = sects * width
 
-    ids = (section_ids * blocks + block_ids).astype(jnp.bfloat16)
-    ids = jnp.broadcast_to(ids.T.reshape(1, entries, 1), (1, entries, points))
+    ids = jnp.tile((section_ids * blocks + block_ids).T.reshape(entries), rups)
+    mine = jnp.arange(points, dtype=jnp.int32) // entries == lax.axis_index("rup")
+    ids = jnp.where(mine, ids, 0).astype(jnp.bfloat16)
+    ids = jnp.broadcast_to(ids.reshape(1, 1, points), (1, entries, points))
     moment = jnp.transpose(moment_tensor, (2, 1, 0, 3)).reshape(comps, entries, points)
     moment = jnp.concatenate([moment, ids])
     moment = jnp.broadcast_to(moment[None], (sects,) + moment.shape)

time: 245 us -> 243 us (level)
  Pallas kernels: 47.5 us -> 44.1 us
  waiting for transfers between devices: 12.6 us -> 15.3 us
    pallas_call x2, Pallas kernels: 36.5 us -> 33.1 us  [contract(): pl.pallas_call(functools.partial(contract_kernel, width, blocks, sub, fir...]
    all_to_all x1, waiting for transfers between devices: 4.37 us -> 6.91 us  [body(): lax.all_to_all(arrived, both, split_axis=0, concat_axis=0, tiled=True)]
  transfers between devices with their start and end apart: 4 -> 4, of which waited for: 2 -> 2; matrix products, arithmetic and copies ran while one was open for 1% -> 1% of each run, Pallas kernels for 15% -> 14%
where the time goes in v5:
time: 243 us
  blocking collectives  145 us (60%)
  Pallas kernels  44.1 us (18%)
  starting transfers between devices  19.6 us (8%)
  waiting for transfers between devices  15.3 us (6%)
  between operations  13.5 us (6%)
  other arithmetic  2.48 us (1%)
  local copies, waits for them, and re-layouts  2.47 us (1%)
    all_to_all x1, blocking collectives, body(): lax.all_to_all(arrived, both, split_axis=0, concat_axis=0, tiled=True)  84.6 us
    all_to_all x1, blocking collectives, body(): lax.all_to_all(green, 'sect', split_axis=0, concat_axis=0, tiled=True)  60.6 us
    pallas_call x2, Pallas kernels, contract(): pl.pallas_call(functools.partial(contract_kernel, width, blocks, sub, fir...  33.1 us
    pallas_call x1, Pallas kernels, split(): pl.pallas_call(functools.partial(split_kernel, len(counts)), in_specs=[an...  9.77 us
    all_to_all x1, starting transfers between devices, body(): lax.all_to_all(moment, 'sect', split_axis=0, concat_axis=0, tiled=True)  8.47 us
    all_to_all x1, waiting for transfers between devices, body(): lax.all_to_all(send, both, split_axis=0, concat_axis=0, tiled=True)  8.4 us
    all_to_all x1, waiting for transfers between devices, body(): lax.all_to_all(arrived, both, split_axis=0, concat_axis=0, tiled=True)  6.91 us
    all_to_all x1, starting transfers between devices, body(): lax.all_to_all(arrived, both, split_axis=0, concat_axis=0, tiled=True)  6.61 us
  transfers between devices with their start and end apart: 4, of which 2 were waited for; matrix products, arithmetic and copies ran while one was open for 1% of the time, Pallas kernels for 14%

profile of v5, /device:TPU:1, one launch (start us, length us, event | category | flops | bytes accessed | tf_op | source)
XLA Modules:
  0.0 242.6 jit_solution(4828031138915838797)
XLA Ops:
  6.5 0.7 add_bitcast_fusion
  7.2 0.1 tile.10
  7.3 0.1 tile.12
  7.4 0.7 copy.14
  8.2 0.8 broadcast_in_dim.7
  9.0 8.5 %all-to-all-start = ((bf16[16,7,16,128]{3,2,1,0:T(8,128)(2,1)}), bf16[16,7,16,128]{3,2,1,0:T(8,128)(2,1)}, u32[]{:S(2)}, u32[]{:S(2)}) async-start(bf16[16,7,16,128]{3,2,1,0:T(8,128)(2,1)} %broadcast_in_dim.7), calls=%async_computation | async-start | bytes 917504 | tf_op jit(solution)/shard_map/all_to_all | solution.py:303
  17.5 0.0 all-gather.3.cloned.1.call-start
  17.5 9.8 %shard_map.100 = (bf16[16,8,6,24,128]{4,3,2,1,0:T(8,128)(2,1)}, bf16[16,8,6,2,16,128]{5,4,3,2,1,0:T(8,128)(2,1)}, bf16[16,8,2,2,16,128]{5,4,3,2,1,0:T(8,128)(2,1)}) custom-call(bf16[8,6,3,16,8,128]{5,4,3,2,1,0:T(8,128)(2,1)} %bitcast.25, bf16[8,2,2,128,8,128]{5,4,3,2,1,0:T(8,128)(2,1)} %bitcast.22), custom_call_target="tpu_custom_call" | custom-call | flops 13107200 | bytes 26214400 | tf_op jit(solution)/shard_map/pallas_call | solution.py:97
  27.3 0.0 all-to-all-done
  27.3 0.0 all-gather.3.cloned.1.call-update
  27.4 60.6 %all_to_all.25.refs_2_ = bf16[16,8,6,24,128]{4,3,2,1,0:T(8,128)(2,1)} all-to-all(bf16[16,8,6,24,128]{4,3,2,1,0:T(8,128)(2,1)} %get-tuple-element.30), channel_id=1, replica_groups=mesh['sect'=16,'rup'=8] {'sect'}, dimensions={0} | all-to-all | bytes 9437184 | tf_op jit(solution)/shard_map/all_to_all | solution.py:312
  87.9 0.0 all-gather.3.cloned.1.call-done
  87.9 84.6 %all_to_all.26 = bf16[128,6,2,16,128]{4,3,2,1,0:T(8,128)(2,1)} all-to-all(bf16[128,6,2,16,128]{4,3,2,1,0:T(8,128)(2,1)} %bitcast.23), channel_id=1, replica_groups=mesh['sect'=16,'rup'=8] {'sect','rup'}, dimensions={0} | all-to-all | bytes 12582912 | tf_op jit(solution)/shard_map/all_to_all | solution.py:325
  172.5 6.6 %all-to-all-start.3 = ((bf16[128,2,2,16,128]{4,3,2,1,0:T(8,128)(2,1)}), bf16[128,2,2,16,128]{4,3,2,1,0:T(8,128)(2,1)}, u32[]{:S(2)}, u32[]{:S(2)}) async-start(bf16[128,2,2,16,128]{4,3,2,1,0:T(8,128)(2,1)} %bitcast.8), calls=%async_computation.3 | async-start | bytes 4194304 | tf_op jit(solution)/shard_map/all_to_all | solution.py:325
  179.1 23.1 %shard_map.101.refs_4_ = f32[128,128]{1,0:T(8,128)} custom-call(bf16[16,8,6,2,16,128]{5,4,3,2,1,0:T(8,128)(2,1)} %bitcast.24, bf16[8,16,7,16,128]{4,3,2,1,0:T(8,128)(2,1)} %bitcast.27, bf16[16,8,6,24,128]{4,3,2,1,0:T(8,128)(2,1)} %all_to_all.25.refs_2_, bf16[2,48,384]{2,1,0:T(8,128)(2,1)} %constant.41.clone.refs_3_), custom_call_target="tpu_custom_call" | custom-call | flops 14495514624 | bytes 9830400 | tf_op jit(solution)/shard_map/pallas_call | solution.py:196
  202.2 6.9 %all-to-all-done.3 = bf16[128,2,2,16,128]{4,3,2,1,0:T(8,128)(2,1)} async-done(((bf16[128,2,2,16,128]{4,3,2,1,0:T(8,128)(2,1)}), bf16[128,2,2,16,128]{4,3,2,1,0:T(8,128)(2,1)}, u32[]{:S(2)}, u32[]{:S(2)}) %all-to-all-start.3) | async-done | bytes 2097184 | tf_op jit(solution)/shard_map/all_to_all | solution.py:325
  209.2 10.0 %shard_map.102 = f32[128,4,128]{2,1,0:T(4,128)} custom-call(bf16[16,8,2,2,16,128]{5,4,3,2,1,0:T(8,128)(2,1)} %bitcast.9.refs_0_, bf16[8,16,7,16,128]{4,3,2,1,0:T(8,128)(2,1)} %bitcast.28, bf16[16,8,6,24,128]{4,3,2,1,0:T(8,128)(2,1)} %all_to_all.25.refs_2_, bf16[2,48,384]{2,1,0:T(8,128)(2,1)} %constant.41.clone.refs_3_, f32[128,128]{1,0:T(8,128)} %shard_map.101.refs_4_), custom_call_target="tpu_custom_call" | custom-call | flops 4831838208 | bytes 3276800 | tf_op jit(solution)/shard_map/pallas_call | solution.py:196
  219.1 4.5 %all-to-all-start.4 = ((f32[128,4,128]{2,1,0:T(4,128)}), f32[128,4,128]{2,1,0:T(4,128)S(1)}, u32[]{:S(2)}, u32[]{:S(2)}) async-start(f32[128,4,128]{2,1,0:T(4,128)} %shard_map.102), calls=%async_computation.4 | async-start | bytes 524288 | tf_op jit(solution)/shard_map/all_to_all | solution.py:337
  223.7 0.7 dynamic-slice_bitcast_fusion
  224.4 1.2 multiply_subtract_fusion
  225.6 0.2 pad_maximum_fusion
  225.8 0.4 fusion
  226.2 8.4 %all-to-all-done.4.spectra_ref = f32[128,4,128]{2,1,0:T(4,128)S(1)} async-done(((f32[128,4,128]{2,1,0:T(4,128)}), f32[128,4,128]{2,1,0:T(4,128)S(1)}, u32[]{:S(2)}, u32[]{:S(2)}) %all-to-all-start.4) | async-done | bytes 262176 | tf_op jit(solution)/shard_map/all_to_all | solution.py:337
  234.6 1.2 shard_map.103
  (4 shorter events, 0.0 us)
Async XLA Ops:
  9.0 18.3 %all-to-all-start = ((bf16[16,7,16,128]{3,2,1,0:T(8,128)(2,1)}), bf16[16,7,16,128]{3,2,1,0:T(8,128)(2,1)}, u32[]{:S(2)}, u32[]{:S(2)}) async-start(bf16[16,7,16,128]{3,2,1,0:T(8,128)(2,1)} %broadcast_in_dim.7), calls=%async_computation | async-start | bytes 917504 | tf_op jit(solution)/shard_map/all_to_all | solution.py:303
  17.5 70.4 %all-gather.3.cloned.1.call-start = ((), (), s32[]{:S(2)}) async-start(), calls=%async_computation.5 | async-start | bytes 4128768 | tf_op jit(solution)/shard_map/all_gather | solution.py:311
  172.5 36.7 %all-to-all-start.3 = ((bf16[128,2,2,16,128]{4,3,2,1,0:T(8,128)(2,1)}), bf16[128,2,2,16,128]{4,3,2,1,0:T(8,128)(2,1)}, u32[]{:S(2)}, u32[]{:S(2)}) async-start(bf16[128,2,2,16,128]{4,3,2,1,0:T(8,128)(2,1)} %bitcast.8), calls=%async_computation.3 | async-start | bytes 4194304 | tf_op jit(solution)/shard_map/all_to_all | solution.py:325
  219.1 15.4 %all-to-all-start.4 = ((f32[128,4,128]{2,1,0:T(4,128)}), f32[128,4,128]{2,1,0:T(4,128)S(1)}, u32[]{:S(2)}, u32[]{:S(2)}) async-start(f32[128,4,128]{2,1,0:T(4,128)} %shard_map.102), calls=%async_computation.4 | async-start | bytes 524288 | tf_op jit(solution)/shard_map/all_to_all | solution.py:337
Sparse Core Ops, SparseCore 0:
  27.5 32.3 all-gather.2

commit v6 on v5

--- a/solution.py
+++ b/solution.py
@@ -163,12 +163,15 @@
 
         @pl.when(f == pl.num_programs(0) - 1)
         def _():
-            owned = out_ref.shape[1]
+            pairs = out_ref.shape[1]
+            owned = 2 * pairs
             turned = sum_ref[...].T.reshape(rups, 2, entries // 2, LANES)
             turned = (turned[:, 0] + turned[:, 1]).reshape(rups * entries // 2, LANES)
+            moved = pltpu.roll(turned, LANES // 2, 1)
             for s in range(sects):
+                mine = turned[s * owned : s * owned + pairs] + moved[s * owned + pairs : (s + 1) * owned]
                 for k in range(rups):
-                    out_ref[s * rups + k] = turned[s * owned : (s + 1) * owned]
+                    out_ref[s * rups + k] = mine
 
 
 def contract(slip, moment, green, fold, prev, first, width, blocks):
@@ -189,7 +192,7 @@
     if final:
         in_specs.append(pl.BlockSpec(prev.shape, lambda f: (0, 0)))
         args.append(prev)
-        shape = (sects * rups, ruptures // sects, LANES)
+        shape = (sects * rups, ruptures // sects // 2, LANES)
         scratch.append(pltpu.VMEM((LANES, LANES), jnp.float32))
     else:
         shape = (LANES, LANES)
@@ -245,8 +248,11 @@
     devices = spectra_ref.shape[0]
     used = 2 * dirs * sub
     rows = left_ref.shape[0]
-    for r in range(owned):
-        turned_ref[r] = spectra_ref[:, r, :].T[:used]
+    pairs = owned // 2
+    for r in range(pairs):
+        turned = spectra_ref[:, r, :].T
+        turned_ref[r] = turned[:used]
+        turned_ref[r + pairs] = turned[LANES // 2 : LANES // 2 + used]
     left_ref[...] = jnp.zeros(left_ref.shape, jnp.float32)
     for part in range(2):
         for f in range(sub):
@@ -267,7 +273,8 @@
 
 
 def transform(spectra, high, low, dirs, sub):
-    devices, owned, lanes = spectra.shape
+    devices, pairs, _ = spectra.shape
+    owned = 2 * pairs
     depth, times = high.shape
     return pl.pallas_call(
         functools.partial(transform_kernel, sub),

time: 243 us -> 242 us (level)
  no operation moved by 1% of the time
where the time goes in v6:
time: 242 us
  blocking collectives  145 us (60%)
  Pallas kernels  44.1 us (18%)
  starting transfers between devices  19.6 us (8%)
  waiting for transfers between devices  14.5 us (6%)
  between operations  13.5 us (6%)
  other arithmetic  2.48 us (1%)
  local copies, waits for them, and re-layouts  2.47 us (1%)
    all_to_all x1, blocking collectives, body(): lax.all_to_all(arrived, both, split_axis=0, concat_axis=0, tiled=True)  84.6 us
    all_to_all x1, blocking collectives, body(): lax.all_to_all(green, 'sect', split_axis=0, concat_axis=0, tiled=True)  60.6 us
    pallas_call x2, Pallas kernels, contract(): pl.pallas_call(functools.partial(contract_kernel, width, blocks, sub, fir...  33.1 us
    pallas_call x1, Pallas kernels, split(): pl.pallas_call(functools.partial(split_kernel, len(counts)), in_specs=[an...  9.77 us
    all_to_all x1, starting transfers between devices, body(): lax.all_to_all(moment, 'sect', split_axis=0, concat_axis=0, tiled=True)  8.47 us
    all_to_all x1, waiting for transfers between devices, body(): lax.all_to_all(send, both, split_axis=0, concat_axis=0, tiled=True)  7.57 us
    all_to_all x1, waiting for transfers between devices, body(): lax.all_to_all(arrived, both, split_axis=0, concat_axis=0, tiled=True)  6.91 us
    all_to_all x1, starting transfers between devices, body(): lax.all_to_all(arrived, both, split_axis=0, concat_axis=0, tiled=True)  6.61 us
  transfers between devices with their start and end apart: 4, of which 2 were waited for; matrix products, arithmetic and copies ran while one was open for 1% of the time, Pallas kernels for 14%

profile of v6, /device:TPU:1, one launch (start us, length us, event | category | flops | bytes accessed | tf_op | source)
XLA Modules:
  0.0 241.8 jit_solution(12994119292451642116)
XLA Ops:
  6.5 0.7 add_bitcast_fusion
  7.2 0.1 tile.10
  7.3 0.1 tile.12
  7.4 0.7 copy.14
  8.2 0.8 broadcast_in_dim.7
  9.0 8.5 %all-to-all-start = ((bf16[16,7,16,128]{3,2,1,0:T(8,128)(2,1)}), bf16[16,7,16,128]{3,2,1,0:T(8,128)(2,1)}, u32[]{:S(2)}, u32[]{:S(2)}) async-start(bf16[16,7,16,128]{3,2,1,0:T(8,128)(2,1)} %broadcast_in_dim.7), calls=%async_computation | async-start | bytes 917504 | tf_op jit(solution)/shard_map/all_to_all | solution.py:310
  17.5 0.0 all-gather.3.cloned.1.call-start
  17.5 9.8 %shard_map.100 = (bf16[16,8,6,24,128]{4,3,2,1,0:T(8,128)(2,1)}, bf16[16,8,6,2,16,128]{5,4,3,2,1,0:T(8,128)(2,1)}, bf16[16,8,2,2,16,128]{5,4,3,2,1,0:T(8,128)(2,1)}) custom-call(bf16[8,6,3,16,8,128]{5,4,3,2,1,0:T(8,128)(2,1)} %bitcast.25, bf16[8,2,2,128,8,128]{5,4,3,2,1,0:T(8,128)(2,1)} %bitcast.22), custom_call_target="tpu_custom_call" | custom-call | flops 13107200 | bytes 26214400 | tf_op jit(solution)/shard_map/pallas_call | solution.py:97
  27.3 0.0 all-to-all-done
  27.3 0.0 all-gather.3.cloned.1.call-update
  27.4 60.6 %all_to_all.25.refs_2_ = bf16[16,8,6,24,128]{4,3,2,1,0:T(8,128)(2,1)} all-to-all(bf16[16,8,6,24,128]{4,3,2,1,0:T(8,128)(2,1)} %get-tuple-element.30), channel_id=1, replica_groups=mesh['sect'=16,'rup'=8] {'sect'}, dimensions={0} | all-to-all | bytes 9437184 | tf_op jit(solution)/shard_map/all_to_all | solution.py:319
  87.9 0.0 all-gather.3.cloned.1.call-done
  87.9 84.6 %all_to_all.26 = bf16[128,6,2,16,128]{4,3,2,1,0:T(8,128)(2,1)} all-to-all(bf16[128,6,2,16,128]{4,3,2,1,0:T(8,128)(2,1)} %bitcast.23), channel_id=1, replica_groups=mesh['sect'=16,'rup'=8] {'sect','rup'}, dimensions={0} | all-to-all | bytes 12582912 | tf_op jit(solution)/shard_map/all_to_all | solution.py:332
  172.5 6.6 %all-to-all-start.3 = ((bf16[128,2,2,16,128]{4,3,2,1,0:T(8,128)(2,1)}), bf16[128,2,2,16,128]{4,3,2,1,0:T(8,128)(2,1)}, u32[]{:S(2)}, u32[]{:S(2)}) async-start(bf16[128,2,2,16,128]{4,3,2,1,0:T(8,128)(2,1)} %bitcast.8), calls=%async_computation.3 | async-start | bytes 4194304 | tf_op jit(solution)/shard_map/all_to_all | solution.py:332
  179.1 23.1 %shard_map.101.refs_4_ = f32[128,128]{1,0:T(8,128)} custom-call(bf16[16,8,6,2,16,128]{5,4,3,2,1,0:T(8,128)(2,1)} %bitcast.24, bf16[8,16,7,16,128]{4,3,2,1,0:T(8,128)(2,1)} %bitcast.27, bf16[16,8,6,24,128]{4,3,2,1,0:T(8,128)(2,1)} %all_to_all.25.refs_2_, bf16[2,48,384]{2,1,0:T(8,128)(2,1)} %constant.41.clone.refs_3_), custom_call_target="tpu_custom_call" | custom-call | flops 14495514624 | bytes 9830400 | tf_op jit(solution)/shard_map/pallas_call | solution.py:199
  202.2 6.9 %all-to-all-done.3 = bf16[128,2,2,16,128]{4,3,2,1,0:T(8,128)(2,1)} async-done(((bf16[128,2,2,16,128]{4,3,2,1,0:T(8,128)(2,1)}), bf16[128,2,2,16,128]{4,3,2,1,0:T(8,128)(2,1)}, u32[]{:S(2)}, u32[]{:S(2)}) %all-to-all-start.3) | async-done | bytes 2097184 | tf_op jit(solution)/shard_map/all_to_all | solution.py:332
  209.2 10.0 %shard_map.102 = f32[128,2,128]{2,1,0:T(2,128)} custom-call(bf16[16,8,2,2,16,128]{5,4,3,2,1,0:T(8,128)(2,1)} %bitcast.9.refs_0_, bf16[8,16,7,16,128]{4,3,2,1,0:T(8,128)(2,1)} %bitcast.28, bf16[16,8,6,24,128]{4,3,2,1,0:T(8,128)(2,1)} %all_to_all.25.refs_2_, bf16[2,48,384]{2,1,0:T(8,128)(2,1)} %constant.41.clone.refs_3_, f32[128,128]{1,0:T(8,128)} %shard_map.101.refs_4_), custom_call_target="tpu_custom_call" | custom-call | flops 4831838208 | bytes 3276800 | tf_op jit(solution)/shard_map/pallas_call | solution.py:199
  219.2 4.5 %all-to-all-start.4 = ((f32[128,2,128]{2,1,0:T(2,128)}), f32[128,2,128]{2,1,0:T(2,128)S(1)}, u32[]{:S(2)}, u32[]{:S(2)}) async-start(f32[128,2,128]{2,1,0:T(2,128)} %shard_map.102), calls=%async_computation.4 | async-start | bytes 262144 | tf_op jit(solution)/shard_map/all_to_all | solution.py:344
  223.7 0.7 dynamic-slice_bitcast_fusion
  224.4 1.2 multiply_subtract_fusion
  225.7 0.2 pad_maximum_fusion
  225.8 0.4 fusion
  226.2 7.6 %all-to-all-done.4.spectra_ref = f32[128,2,128]{2,1,0:T(2,128)S(1)} async-done(((f32[128,2,128]{2,1,0:T(2,128)}), f32[128,2,128]{2,1,0:T(2,128)S(1)}, u32[]{:S(2)}, u32[]{:S(2)}) %all-to-all-start.4) | async-done | bytes 131104 | tf_op jit(solution)/shard_map/all_to_all | solution.py:344
  233.8 1.2 shard_map.103
  (4 shorter events, 0.0 us)
Async XLA Ops:
  9.0 18.3 %all-to-all-start = ((bf16[16,7,16,128]{3,2,1,0:T(8,128)(2,1)}), bf16[16,7,16,128]{3,2,1,0:T(8,128)(2,1)}, u32[]{:S(2)}, u32[]{:S(2)}) async-start(bf16[16,7,16,128]{3,2,1,0:T(8,128)(2,1)} %broadcast_in_dim.7), calls=%async_computation | async-start | bytes 917504 | tf_op jit(solution)/shard_map/all_to_all | solution.py:310
  17.5 70.4 %all-gather.3.cloned.1.call-start = ((), (), s32[]{:S(2)}) async-start(), calls=%async_computation.5 | async-start | bytes 4128768 | tf_op jit(solution)/shard_map/all_gather | solution.py:318
  172.5 36.7 %all-to-all-start.3 = ((bf16[128,2,2,16,128]{4,3,2,1,0:T(8,128)(2,1)}), bf16[128,2,2,16,128]{4,3,2,1,0:T(8,128)(2,1)}, u32[]{:S(2)}, u32[]{:S(2)}) async-start(bf16[128,2,2,16,128]{4,3,2,1,0:T(8,128)(2,1)} %bitcast.8), calls=%async_computation.3 | async-start | bytes 4194304 | tf_op jit(solution)/shard_map/all_to_all | solution.py:332
  219.2 14.6 %all-to-all-start.4 = ((f32[128,2,128]{2,1,0:T(2,128)}), f32[128,2,128]{2,1,0:T(2,128)S(1)}, u32[]{:S(2)}, u32[]{:S(2)}) async-start(f32[128,2,128]{2,1,0:T(2,128)} %shard_map.102), calls=%async_computation.4 | async-start | bytes 262144 | tf_op jit(solution)/shard_map/all_to_all | solution.py:344
Sparse Core Ops, SparseCore 0:
  27.5 32.3 all-gather.2
